TPU v7x, 256 devices: a whole 4x4x8 slice. The times are simulated.
256 devices in a mesh: ctx: 16 (over x, y), exp: 16 (over z, core).
Axes of the slice: x: 4, y: 4, z: 8, core: 2. Of those that a mesh axis runs over, the one named last changes fastest.
Arguments:
- inner_input: bfloat16 [2048, 8192], P('ctx', 'exp'), may hold values from -6 to 6
- gate_input: bfloat16 [2048, 8192], P('ctx', 'exp'), may hold values from -6 to 6
- step_codes: int32 [2048, 8192], P('ctx', 'exp'), may hold values from 4 to 16384
- conv_weight: float32 [4, 8192], P(None, 'exp'), may hold values from -3 to 3
- conv_bias: float32 [8192], P('exp'), may hold values from -3 to 3
- decay_rates: float32 [16, 8192], P(None, 'exp')
- skip_gain: float32 [8192], P('exp'), may hold values from 0.5 to 1.5
- state_proj: bfloat16 [8192, 32], P('exp'), may hold values from -0.0625 to 0.0625
- out_proj: bfloat16 [8192, 4096], P('exp'), may hold values from -0.0625 to 0.0625
- residual: bfloat16 [2048, 4096], P(('ctx', 'exp')), may hold values from -6 to 6
- norm_gain: float32 [4096], replicated, may hold values from 0.25 to 1.75
- expert_ids: int32 [2048, 2], P(('ctx', 'exp')), may hold values from 0 to 15, all different within a row; in each aligned block of 8 rows (0 to 7, 8 to 15, ...) at most 2 rows name the same one
- gate_codes: int32 [2048, 2], P(('ctx', 'exp')), may hold values from 1 to 255
- up_weight: bfloat16 [16, 4096, 8192], P('exp', None, 'ctx'), may hold values from -0.09375 to 0.09375
- down_weight: bfloat16 [16, 8192, 4096], P('exp', 'ctx'), may hold values from -0.0625 to 0.0625
Outputs:
- layer_out: bfloat16 [2048, 4096], P(('ctx', 'exp'))
Inputs may be any that keep to these rules, and one draw needn't show every extreme that they name: `expert_ids`: each row names 2 different experts. In each aligned block of 8 rows (the tokens of one device) no expert is named by more than 2 rows.
All inputs are finite; a program needn't handle non-finite values.
Results may differ from a plain program's by a relative error of at most 0.028.
Values may be sent and summed in bfloat16 or wider, within the bound.
No kernel may reach another device: no remote copies, remote signals or barrier semaphores. Data moves between devices by JAX's collectives and lax.ppermute only.
A program may use at most 128 MiB of HBM per device.

v0:
```python
import functools
import math
import jax
import jax.numpy as jnp
from jax import lax
from jax.experimental import pallas as pl
from jax.experimental.pallas import tpu as pltpu
from jax.sharding import PartitionSpec as P

F32 = jnp.float32
BF16 = jnp.bfloat16
SIDE_X, SIDE_Y = 4, 4
DEPTH, CORES = 8, 2
GROUP = 8
SPAN = 32
VMEM = pl.BlockSpec(memory_space=pltpu.VMEM)
HBM = pl.BlockSpec(memory_space=pltpu.HBM)
SMALL = pltpu.CompilerParams(vmem_limit_bytes=8 * 1024 * 1024)
MEDIUM = pltpu.CompilerParams(vmem_limit_bytes=20 * 1024 * 1024)


def shifted(array, axis, by):
    count = lax.axis_size(axis)
    pairs = [(i, i + by) for i in range(count) if 0 <= i + by < count]
    return lax.ppermute(array, axis, pairs)


def along_plane(array, dx, dy):
    pairs = [
        (x * SIDE_Y + y, (x + dx) % SIDE_X * SIDE_Y + (y + dy) % SIDE_Y)
        for x in range(SIDE_X)
        for y in range(SIDE_Y)
    ]
    return lax.ppermute(array, "ctx", pairs)


def along_depth(array, target):
    pairs = []
    for z in range(DEPTH):
        for c in range(CORES):
            to_z, to_c = target(z, c)
            pairs.append((z * CORES + c, to_z % DEPTH * CORES + to_c))
    return lax.ppermute(array, "exp", pairs)


def near(array):
    return [
        along_depth(array, lambda z, c: (z, 1 - c)),
        along_depth(array, lambda z, c: (z ^ 1, c)),
        along_depth(array, lambda z, c: (z ^ 1, 1 - c)),
    ]


def far(arrays):
    return [along_depth(a, lambda z, c, k=k: (z + 2 * k, c)) for k, a in enumerate(arrays) if k]


def silu(v):
    return v / (1.0 + jnp.exp(-v))


def stage_kernel(
    inner_ref, codes_ref, gate_ref, taps_ref, bias_ref, proj_ref, rates_ref, skip_ref,
    conv_out, codes_out, gate_out, taps_out, proj_out, rates_out, skip_out,
    inner, codes, gate, bias, rates, padded, sems,
):
    moves = [
        (inner_ref, inner),
        (taps_ref, taps_out),
        (bias_ref, bias),
        (codes_ref, codes),
        (gate_ref, gate),
        (proj_ref, proj_out),
        (rates_ref, rates),
        (skip_ref, skip_out),
    ]
    copies = [pltpu.make_async_copy(a, b, sems.at[k]) for k, (a, b) in enumerate(moves)]
    for copy in copies:
        copy.start()
    length = inner.shape[0]
    count = taps_out.shape[0]
    padded[0:8, :] = jnp.zeros((8, padded.shape[1]), F32)
    for copy in copies[:3]:
        copy.wait()
    padded[8:, :] = inner[...].astype(F32)
    total = taps_out[0:1, :] * padded[8 - count + 1 : 8 - count + 1 + length, :]
    for k in range(1, count):
        start = 8 - count + 1 + k
        total = total + taps_out[k : k + 1, :] * padded[start : start + length, :]
    conv_out[...] = total + bias[...]
    for copy in copies[3:]:
        copy.wait()
    codes_out[...] = codes[...].astype(F32)
    gate_out[...] = silu(gate[...].astype(F32))
    rates_out[...] = rates[...] * (-math.log2(math.e) / 256.0)


def signal_kernel(border_ref, conv_ref, codes_ref, taps_ref, proj_ref, signal_ref, drive_ref, maps_ref):
    count = taps_ref.shape[0]
    width = conv_ref.shape[1]
    border = border_ref[...].astype(F32)
    rows = lax.broadcasted_iota(jnp.int32, (8, width), 0)
    first = jnp.zeros((8, width), F32)
    for t in range(count - 1):
        row = jnp.zeros((1, width), F32)
        for k in range(count - 1 - t):
            row = row + taps_ref[k : k + 1, :] * border[t + k : t + k + 1, :]
        first = jnp.where(rows == t, row, first)
    signal_ref[...] = silu(conv_ref[...])
    signal_ref[0:8, :] = silu(conv_ref[0:8, :] + first)
    signal = signal_ref[...]
    drive_ref[...] = jnp.minimum(codes_ref[...] * (1.0 / 256.0), 1.0) * signal
    maps_ref[...] = lax.dot_general(
        proj_ref[...],
        signal.astype(BF16),
        (((1,), (1,)), ((), ())),
        preferred_element_type=F32,
    )


def recur(maps_ref, codes_ref, drive_ref, rates, state, out_ref):
    width = codes_ref.shape[1]
    count = rates.shape[0]
    tiles = width // 128

    def group(g, state):
        rows = pl.ds(pl.multiple_of(g * SPAN, SPAN), SPAN)
        codes = codes_ref[rows, :]
        drive = drive_ref[rows, :]
        lanes = maps_ref.shape[1]
        maps = pltpu.roll(maps_ref[...], (lanes - g * SPAN) % lanes, 1)
        outs = []
        for k in range(SPAN):
            into = jnp.broadcast_to(maps[:count, k : k + 1], (count, 128))
            if out_ref is not None:
                out_of = jnp.broadcast_to(maps[count:, k : k + 1], (count, 128))
            pieces = []
            new = []
            for i in range(tiles):
                cols = slice(i * 128, (i + 1) * 128)
                decay = jnp.exp2(codes[k : k + 1, cols] * rates[:, cols])
                now = decay * state[i] + into * drive[k : k + 1, cols]
                new.append(now)
                if out_ref is not None:
                    pieces.append(jnp.sum(out_of * now, axis=0, keepdims=True))
            state = tuple(new)
            if out_ref is not None:
                outs.append(jnp.concatenate(pieces, axis=1))
        if out_ref is not None:
            out_ref[rows, :] = jnp.concatenate(outs, axis=0)
        return state

    return lax.fori_loop(0, codes_ref.shape[0] // SPAN, group, state)


def end_kernel(a_ref, b_ref, c_ref, d_ref, codes_ref, drive_ref, rates_ref, maps_ref, sent_ref):
    maps_ref[...] = (a_ref[...] + b_ref[...]) + (c_ref[...] + d_ref[...])
    rates = rates_ref[...]
    count, width = rates.shape
    zero = tuple(jnp.zeros((count, 128), F32) for _ in range(width // 128))
    state = jnp.concatenate(recur(maps_ref, codes_ref, drive_ref, rates, zero, None), axis=1)
    sent_ref[...] = packed(state, jnp.sum(codes_ref[...], axis=0, keepdims=True))


def packed(state, total):
    rows = lax.broadcasted_iota(jnp.int32, state.shape, 0)
    parts = jnp.zeros(state.shape, F32)
    for i in range(3):
        part = total.astype(BF16).astype(F32)
        parts = jnp.where(rows == i, part, parts)
        total = total - part
    return jnp.concatenate([state, parts], axis=0).astype(BF16)


def unpacked(ref, k, count):
    block = ref[pl.ds(pl.multiple_of(k * 2 * count, 2 * count), 2 * count), :].astype(F32)
    return block[:count], block[count : count + 1] + block[count + 1 : count + 2] + block[count + 2 : count + 3]


def follow(ref, k, rates, state):
    end, total = unpacked(ref, k, rates.shape[0])
    return jnp.exp2(total * rates) * state + end


def line_kernel(a_ref, b_ref, c_ref, d_ref, rates_ref, ends_ref, sent_ref):
    rates = rates_ref[...]
    count, width = rates.shape
    for k, ref in enumerate((a_ref, b_ref, c_ref, d_ref)):
        ends_ref[2 * count * k : 2 * count * (k + 1), :] = ref[...]
    y = lax.axis_index("ctx") % SIDE_Y

    def one(j, carry):
        state, total = carry
        at = (y + SIDE_Y - j) % SIDE_Y
        end, more = unpacked(ends_ref, at, count)
        return jnp.exp2(more * rates) * state + end, total + more

    state, total = lax.fori_loop(
        0, SIDE_Y, one, (jnp.zeros((count, width), F32), jnp.zeros((1, width), F32))
    )
    sent_ref[...] = packed(state, total)


def scan_kernel(
    rows_ref, ends_ref, maps_ref, codes_ref, drive_ref, signal_ref, rates_ref, skip_ref, gate_ref, proj_ref,
    own_ref, other_ref, out, arranged, gated, proj, sem,
):
    fetch = pltpu.make_async_copy(proj_ref, proj, sem)
    fetch.start()
    rates = rates_ref[...]
    count, width = rates.shape
    ctx, exp = lax.axis_index("ctx"), lax.axis_index("exp")
    x, y = ctx // SIDE_Y, ctx % SIDE_Y

    zero = jnp.zeros((count, width), F32)
    start = lax.fori_loop(0, x, lambda j, state: follow(rows_ref, (x - j), rates, state), zero)
    start = lax.fori_loop(0, y, lambda j, state: follow(ends_ref, (y - j), rates, state), start)
    state = tuple(start[:, i * 128 : (i + 1) * 128] for i in range(width // 128))
    recur(maps_ref, codes_ref, drive_ref, rates, state, out)
    z, c = exp // CORES, exp % CORES

    def gate(j, carry):
        rows = pl.ds(pl.multiple_of(j * GROUP, GROUP), GROUP)
        away = (j // CORES + DEPTH - z) % DEPTH
        to = (j % CORES + c) % CORES * DEPTH + away % 2 * (DEPTH // 2) + away // 2
        value = out[rows, :] + skip_ref[...] * signal_ref[rows, :]
        arranged[pl.ds(pl.multiple_of(to * GROUP, GROUP), GROUP), :] = value * gate_ref[rows, :]
        return carry

    lax.fori_loop(0, codes_ref.shape[0] // GROUP, gate, 0)
    gated[...] = arranged[...].astype(BF16)
    fetch.wait()
    half = own_ref.shape[0]
    step = 512

    def product(k, carry):
        cols = pl.ds(pl.multiple_of(k * step, step), step)
        block = jnp.dot(gated[...], proj[:, cols], preferred_element_type=F32)
        own_ref[:, cols] = block[:half].astype(BF16)
        other_ref[:, cols] = block[half:].astype(BF16)
        return carry

    lax.fori_loop(0, proj.shape[1] // step, product, 0)


def state_space(
    inner_input, gate_input, step_codes, conv_weight, conv_bias, decay_rates, skip_gain, state_proj, out_proj
):
    length, width = inner_input.shape
    taps = conv_weight.shape[0]
    count = decay_rates.shape[0]
    model = out_proj.shape[1]
    border = shifted(inner_input[length - taps + 1 :], "ctx", 1)

    def wide(rows, kind=F32):
        return jax.ShapeDtypeStruct((rows, width), kind)

    maps_shape = jax.ShapeDtypeStruct((2 * count, length), F32)
    conv, codes, gate, taps_in, proj, rates, skip = pl.pallas_call(
        stage_kernel,
        out_shape=(
            wide(length), wide(length), wide(length), wide(taps), wide(2 * count, BF16), wide(count), wide(1),
        ),
        in_specs=[HBM] * 8,
        out_specs=(VMEM,) * 7,
        scratch_shapes=[
            pltpu.VMEM((length, width), BF16),
            pltpu.VMEM((length, width), jnp.int32),
            pltpu.VMEM((length, width), BF16),
            pltpu.VMEM((1, width), F32),
            pltpu.VMEM((count, width), F32),
            pltpu.VMEM((length + 8, width), F32),
            pltpu.SemaphoreType.DMA((8,)),
        ],
        compiler_params=SMALL,
        cost_estimate=pl.CostEstimate(flops=1 << 20, bytes_accessed=8 << 20, transcendentals=1 << 16),
        name="stage",
    )(
        *in_hbm(
            inner_input,
            step_codes,
            gate_input,
            conv_weight,
            conv_bias[None],
            state_proj.T,
            decay_rates,
            skip_gain[None],
        )
    )
    signal, drive, part = pl.pallas_call(
        signal_kernel,
        out_shape=(wide(length), wide(length), maps_shape),
        in_specs=[VMEM] * 5,
        out_specs=(VMEM,) * 3,
        compiler_params=SMALL,
        name="signal",
    )(border, conv, codes, taps_in, proj)
    part = sum(near(part), part)
    maps, sent = pl.pallas_call(
        end_kernel,
        out_shape=(maps_shape, wide(2 * count, BF16)),
        in_specs=[VMEM] * 7,
        out_specs=(VMEM,) * 2,
        compiler_params=SMALL,
        name="end_state",
    )(part, *far([part] * (DEPTH // 2)), codes, drive, rates)
    ends, line = pl.pallas_call(
        line_kernel,
        out_shape=(wide(2 * count * SIDE_Y, BF16), wide(2 * count, BF16)),
        in_specs=[VMEM] * 5,
        out_specs=(VMEM,) * 2,
        compiler_params=SMALL,
        name="line",
    )(sent, *[along_plane(sent, 0, k) for k in range(1, SIDE_Y)], rates)
    rows = join([line] + [along_plane(line, k, 0) for k in range(1, SIDE_X)])
    half = jax.ShapeDtypeStruct((length // 2, model), BF16)
    return pl.pallas_call(
        scan_kernel,
        out_shape=(half, half),
        in_specs=[VMEM] * 9 + [HBM],
        out_specs=(VMEM,) * 2,
        scratch_shapes=[
            pltpu.VMEM((length, width), F32),
            pltpu.VMEM((length, width), F32),
            pltpu.VMEM((length, width), BF16),
            pltpu.VMEM((width, model), BF16),
            pltpu.SemaphoreType.DMA,
        ],
        compiler_params=MEDIUM,
        name="scan",
    )(rows, ends, maps, codes, drive, signal, rates, skip, gate, *in_hbm(out_proj))


def join_kernel(*refs):
    out = refs[-1]
    at = 0
    for ref in refs[:-1]:
        out[at : at + ref.shape[0], :] = ref[...]
        at += ref.shape[0]


def join(arrays):
    rows = sum(a.shape[0] for a in arrays)
    return pl.pallas_call(
        join_kernel,
        out_shape=jax.ShapeDtypeStruct((rows,) + arrays[0].shape[1:], arrays[0].dtype),
        in_specs=[VMEM] * len(arrays),
        out_specs=VMEM,
        compiler_params=SMALL,
        name="join",
    )(*arrays)


def in_hbm(*arrays):
    return [pltpu.with_memory_space_constraint(a, pltpu.HBM) for a in arrays]


def added(*arrays):
    return sum(a.astype(F32) for a in arrays).astype(BF16)


def sum_out(own, other):
    pair = added(own, along_depth(other, lambda z, c: (z, 1 - c)))
    even, up, down = pair[: 4 * GROUP], pair[4 * GROUP : 6 * GROUP], pair[6 * GROUP :]
    low = split(along_depth(up, lambda z, c: (z + 1, c)), 2)
    high = split(along_depth(down, lambda z, c: (z - 1, c)), 2)
    even = split(even, 4)
    blocks = [added(even[0], low[0], high[1]), added(even[1], low[1]), even[2], added(even[3], high[0])]
    return sum((a.astype(F32) for a in far(blocks)), blocks[0].astype(F32))


def expert_kernel(count, *refs):
    pieces, (up_ref, down_ref), outs = refs[:count], refs[count : count + 2], refs[count + 2 : 2 * count + 2]
    rows, hidden = refs[2 * count + 2 :]
    step = 256
    places = []
    at = 0
    for ref in pieces:
        places.append(slice(at, at + ref.shape[0]))
        rows[places[-1], :] = ref[...]
        at += ref.shape[0]
    for k in range(up_ref.shape[1] // step):
        cols = slice(k * step, (k + 1) * step)
        block = jnp.dot(rows[...], up_ref[:, cols], preferred_element_type=F32)
        hidden[:, cols] = silu(block).astype(BF16)

    def down(k, carry):
        cols = pl.ds(pl.multiple_of(k * step, step), step)
        block = jnp.dot(hidden[...], down_ref[:, cols], preferred_element_type=F32).astype(BF16)
        for place, out in zip(places, outs):
            out[:, cols] = block[place]
        return carry

    lax.fori_loop(0, down_ref.shape[1] // step, down, 0)


def expert(pieces, up, down):
    size = sum(p.shape[0] for p in pieces)
    model, width = up.shape
    return pl.pallas_call(
        functools.partial(expert_kernel, len(pieces)),
        out_shape=tuple(jax.ShapeDtypeStruct(p.shape, BF16) for p in pieces),
        in_specs=[VMEM] * (len(pieces) + 2),
        out_specs=(VMEM,) * len(pieces),
        scratch_shapes=[pltpu.VMEM((size, model), BF16), pltpu.VMEM((size, width), BF16)],
        compiler_params=MEDIUM,
        cost_estimate=pl.CostEstimate(
            flops=4 * size * model * width, bytes_accessed=4 * size * model, transcendentals=size * width
        ),
        name="expert",
    )(*pieces, up, down)


def fetch_kernel(after_ref, up_ref, down_ref, up_out, down_out, sems):
    up = pltpu.make_async_copy(up_ref, up_out, sems.at[0])
    down = pltpu.make_async_copy(down_ref, down_out, sems.at[1])
    up.start()
    down.start()
    up.wait()
    down.wait()


def fetch(after, up, down):
    return pl.pallas_call(
        fetch_kernel,
        out_shape=(jax.ShapeDtypeStruct(up.shape, BF16), jax.ShapeDtypeStruct(down.shape, BF16)),
        in_specs=[pl.BlockSpec(memory_space=pl.ANY), HBM, HBM],
        out_specs=(VMEM, VMEM),
        scratch_shapes=[pltpu.SemaphoreType.DMA((2,))],
        compiler_params=SMALL,
        cost_estimate=pl.CostEstimate(flops=0, bytes_accessed=32 << 20, transcendentals=0),
        name="fetch",
    )(after, *in_hbm(up, down))


def split(array, parts):
    size = array.shape[0] // parts
    return [array[k * size : (k + 1) * size] for k in range(parts)]


def swap(array):
    return along_depth(array, lambda z, c: (z, 1 - c))


def along_side(array, side, step):
    pairs = []
    for x in range(SIDE_X):
        for y in range(SIDE_Y):
            for exp in range(DEPTH * CORES):
                if (side + exp) % 2 == 0:
                    to = (x + step) % SIDE_X * SIDE_Y + y
                else:
                    to = x * SIDE_Y + (y + step) % SIDE_Y
                pairs.append(((x * SIDE_Y + y) * DEPTH * CORES + exp, to * DEPTH * CORES + exp))
    return lax.ppermute(array, ("ctx", "exp"), pairs)


def run_expert(mine, theirs, up, down):
    steps = (1, 2, 3)
    base = jnp.concatenate([mine, theirs])
    size = mine.shape[0]
    visits = [base] + [along_side(base, 0, k) for k in steps]
    group = join([v[:size] for v in visits] + [v[size:] for v in visits])
    half = group.shape[0] // 2
    after, before = along_side(group, 1, 1), along_side(group, 1, -1)
    up, down = fetch(group, up, down)
    own_mine, own_swapped = expert([group[:half], swap(group[half:])], up, down)
    after, before, up, down, own_mine, own_swapped = lax.optimization_barrier(
        (after, before, up, down, own_mine, own_swapped)
    )
    far_mine = along_side(after[:half], 1, 1)
    far_theirs = along_side(before[half:], 1, -1)
    close = [after[:half], before[:half], swap(after[half:]), swap(before[half:])]
    far_mine, far_swapped = expert([far_mine, swap(far_theirs)], up, down)
    passed = along_side(far_mine, 1, -1), along_side(swap(far_swapped), 1, 1)
    after_mine, before_mine, after_swapped, before_swapped = expert(close, up, down)
    own_theirs, after_theirs, before_theirs = swap(own_swapped), swap(after_swapped), swap(before_swapped)
    one = along_side(jnp.concatenate([added(after_mine, passed[0]), after_theirs]), 1, -1)
    three = along_side(jnp.concatenate([before_mine, added(before_theirs, passed[1])]), 1, 1)
    total_mine = split(added(own_mine, one[:half], three[:half]), 4)
    total_theirs = split(added(own_theirs, one[half:], three[half:]), 4)
    blocks = [jnp.concatenate([m, t]) for m, t in zip(total_mine, total_theirs)]
    return added(blocks[0], *[along_side(blocks[k], 0, -k) for k in steps])


def shards(
    inner_input,
    gate_input,
    step_codes,
    conv_weight,
    conv_bias,
    decay_rates,
    skip_gain,
    state_proj,
    out_proj,
    residual,
    norm_gain,
    expert_ids,
    gate_codes,
    up_weight,
    down_weight,
):
    own, other = state_space(
        inner_input,
        gate_input,
        step_codes,
        conv_weight,
        conv_bias,
        decay_rates,
        skip_gain,
        state_proj,
        out_proj,
    )
    row_count = residual.shape[0]
    mamba_out = sum_out(own, other)
    stream = (residual.astype(F32) + mamba_out).astype(BF16)
    stream_wide = stream.astype(F32)
    normed = (
        stream_wide
        * lax.rsqrt(jnp.mean(stream_wide * stream_wide, axis=-1, keepdims=True) + 1e-05)
        * norm_gain
    ).astype(BF16)
    experts = lax.axis_size("exp") * up_weight.shape[0]
    top_count = expert_ids.shape[1]
    capacity = max(2, 4 * row_count // experts)
    onehot = (
        (expert_ids[:, :, None] == jnp.arange(experts)[None, None, :])
        .astype(jnp.int32)
        .reshape(row_count * top_count, experts)
    )
    before = jnp.cumsum(onehot, axis=0) - onehot
    ranking = jnp.sum(before * onehot, axis=1).reshape(row_count, top_count)
    slot_index = expert_ids // CORES * (CORES * capacity) + ranking * CORES
    slot_index = slot_index + (expert_ids % CORES != ranking).astype(jnp.int32)
    slots = slot_index[:, :, None] == jnp.arange(experts * capacity)[None, None, :]
    dispatch_table = jnp.any(slots, axis=1).astype(BF16)
    up_local = up_weight[0]
    down_local = down_weight[0]
    outgoing = lax.dot_general(
        dispatch_table, normed, (((0,), (0,)), ((), ())), preferred_element_type=F32
    ).astype(BF16)
    outgoing = outgoing.reshape(experts, capacity, -1)
    arrived = lax.all_to_all(outgoing, "exp", split_axis=0, concat_axis=0, tiled=True)
    expert_out = run_expert(arrived[:, 0], arrived[:, 1], up_local, down_local)
    expert_out = jnp.stack(split(expert_out, 2), axis=1)
    returned = lax.all_to_all(expert_out, "exp", split_axis=0, concat_axis=0, tiled=True)
    returned = returned.reshape(experts * capacity, -1)
    gate_weights = gate_codes.astype(F32)
    gate_weights = gate_weights / jnp.sum(gate_weights, axis=1, keepdims=True)
    table = jnp.sum(gate_weights[:, :, None] * slots.astype(F32), axis=1)
    mixture_out = jnp.dot(table, returned.astype(F32), precision=lax.Precision.HIGHEST)
    return (stream_wide + mixture_out).astype(BF16)


def solution(mesh):
    return jax.shard_map(
        shards,
        mesh=mesh,
        in_specs=(
            P("ctx", "exp"),
            P("ctx", "exp"),
            P("ctx", "exp"),
            P(None, "exp"),
            P("exp"),
            P(None, "exp"),
            P("exp"),
            P("exp", None),
            P("exp", None),
            P(("ctx", "exp"), None),
            P(),
            P(("ctx", "exp"), None),
            P(("ctx", "exp"), None),
            P("exp", None, "ctx"),
            P("exp", "ctx", None),
        ),
        out_specs=P(("ctx", "exp"), None),
        check_vma=False,
    )
```

profile of v0, /device:TPU:1, one launch (start us, length us, event | category | flops | bytes accessed | tf_op | source)
XLA Modules:
  0.0 194.8 jit_solution(12411053237753851481)
XLA Ops:
  0.0 0.7 slice.124
  0.7 4.0 %collective-permute-start = (bf16[3,512]{1,0:T(4,128)(2,1)S(1)}, bf16[3,512]{1,0:T(4,128)(2,1)S(1)}, u32[]{:S(2)}, u32[]{:S(2)}) collective-permute-start(bf16[3,512]{1,0:T(4,128)(2,1)S(1)} %slice.124), channel_id=1, source_target_pairs={{0,16},{16,32},{32,48},{48,64},{64,80},{80,96},{96,112},{112,128},... | collective-permute-start | bytes 9224 | tf_op jit(solution)/shard_map/ppermute | solution.py:25
  4.7 1.3 stage.1
  6.3 1.0 collective-permute-start.1
  7.2 1.7 collective-permute-start.2
  9.0 1.0 collective-permute-done.2
  10.0 2.1 %collective-permute-done.3 = f32[32,128]{1,0:T(8,128)S(1)} collective-permute-done((f32[32,128]{1,0:T(8,128)S(1)}, f32[32,128]{1,0:T(8,128)S(1)}, u32[]{:S(2)}, u32[]{:S(2)}) %collective-permute-start.3) | collective-permute-done | bytes 16416 | tf_op jit(solution)/shard_map/ppermute | solution.py:43
  12.1 3.0 %collective-permute-start.4 = (f32[32,128]{1,0:T(8,128)S(1)}, f32[32,128]{1,0:T(8,128)S(1)}, u32[]{:S(2)}, u32[]{:S(2)}) collective-permute-start(f32[32,128]{1,0:T(8,128)S(1)} %add_add_fusion.a_ref), channel_id=1, source_target_pairs={{0,4},{1,5},{2,6},{3,7},{4,8},{5,9},{6,10},{7,11},{8,12},{9,13},{1... | collective-permute-start | bytes 49160 | tf_op jit(solution)/shard_map/ppermute | solution.py:43
  15.1 4.2 %collective-permute-start.5 = (f32[32,128]{1,0:T(8,128)S(1)}, f32[32,128]{1,0:T(8,128)S(1)}, u32[]{:S(2)}, u32[]{:S(2)}) collective-permute-start(f32[32,128]{1,0:T(8,128)S(1)} %add_add_fusion.a_ref), channel_id=1, source_target_pairs={{0,8},{1,9},{2,10},{3,11},{4,12},{5,13},{6,14},{7,15},{8,0},{9,1},... | collective-permute-start | bytes 49160 | tf_op jit(solution)/shard_map/ppermute | solution.py:43
  19.3 2.4 %collective-permute-start.6 = (f32[32,128]{1,0:T(8,128)S(1)}, f32[32,128]{1,0:T(8,128)S(1)}, u32[]{:S(2)}, u32[]{:S(2)}) collective-permute-start(f32[32,128]{1,0:T(8,128)S(1)} %add_add_fusion.a_ref), channel_id=1, source_target_pairs={{0,12},{1,13},{2,14},{3,15},{4,0},{5,1},{6,2},{7,3},{8,4},{9,5},{1... | collective-permute-start | bytes 49160 | tf_op jit(solution)/shard_map/ppermute | solution.py:43
  21.7 1.3 collective-permute-done.6.d_ref
  23.0 1.2 end_state.1
  24.1 2.1 %collective-permute-start.7 = (bf16[32,512]{1,0:T(8,128)(2,1)S(1)}, bf16[32,512]{1,0:T(8,128)(2,1)S(1)}, u32[]{:S(2)}, u32[]{:S(2)}) collective-permute-start(bf16[32,512]{1,0:T(8,128)(2,1)S(1)} %get-tuple-element.44.a_ref), channel_id=1, source_target_pairs={{0,16},{16,32},{32,48},{48,0},{64,80},{80,96},{96,112},{112,64},{1... | collective-permute-start | bytes 98312 | tf_op jit(solution)/shard_map/ppermute | solution.py:34
  26.2 2.6 %collective-permute-start.8 = (bf16[32,512]{1,0:T(8,128)(2,1)S(1)}, bf16[32,512]{1,0:T(8,128)(2,1)S(1)}, u32[]{:S(2)}, u32[]{:S(2)}) collective-permute-start(bf16[32,512]{1,0:T(8,128)(2,1)S(1)} %get-tuple-element.44.a_ref), channel_id=1, source_target_pairs={{0,32},{16,48},{32,0},{48,16},{64,96},{80,112},{96,64},{112,80},{1... | collective-permute-start | bytes 98312 | tf_op jit(solution)/shard_map/ppermute | solution.py:34
  28.8 1.1 collective-permute-start.9
  30.5 1.1 collective-permute-done.9.d_ref
  31.7 1.6 collective-permute-start.10
  33.3 2.5 %collective-permute-start.11 = (bf16[32,512]{1,0:T(8,128)(2,1)S(1)}, bf16[32,512]{1,0:T(8,128)(2,1)S(1)}, u32[]{:S(2)}, u32[]{:S(2)}) collective-permute-start(bf16[32,512]{1,0:T(8,128)(2,1)S(1)} %get-tuple-element.45.refs_0_), channel_id=1, source_target_pairs={{0,128},{16,144},{32,160},{48,176},{64,192},{80,208},{96,224},{112... | collective-permute-start | bytes 98312 | tf_op jit(solution)/shard_map/ppermute | solution.py:34
  35.8 1.2 collective-permute-start.12
  36.9 0.7 collective-permute-done.11.refs_2_
  37.6 0.9 collective-permute-done.12.refs_3_
  38.6 4.3 %scan.1 = (bf16[64,4096]{1,0:T(8,128)(2,1)S(1)}, bf16[64,4096]{1,0:T(8,128)(2,1)S(1)}) custom-call(bf16[128,512]{1,0:T(8,128)(2,1)S(1)} %join.2.rows_ref, bf16[128,512]{1,0:T(8,128)(2,1)S(1)} %get-tuple-element.46.ends_ref, f32[32,128]{1,0:T(8,128)S(1)} %get-tuple-element.47.maps_ref, f32[128,512]{1,0:T(8,128)S(1)} %get-tuple-element.38.codes_ref, ...), custom_call_target="tpu_custom_call" | custom-call | tf_op jit(solution)/shard_map/scan/pallas_call | solution.py:317
  42.9 5.1 %collective-permute-start.13 = (bf16[64,4096]{1,0:T(8,128)(2,1)S(1)}, bf16[64,4096]{1,0:T(8,128)(2,1)S(1)}, u32[]{:S(2)}, u32[]{:S(2)}) collective-permute-start(bf16[64,4096]{1,0:T(8,128)(2,1)S(1)} %get-tuple-element.52), channel_id=1, source_target_pairs={{0,1},{1,0},{2,3},{3,2},{4,5},{5,4},{6,7},{7,6},{8,9},{9,8},{10,11... | collective-permute-start | bytes 1572872 | tf_op jit(solution)/shard_map/ppermute | solution.py:43
  48.5 1.0 collective-permute-done.13
  49.7 0.8 collective-permute-start.14
  50.5 2.5 %collective-permute-start.15 = (bf16[16,4096]{1,0:T(8,128)(2,1)S(1)}, bf16[16,4096]{1,0:T(8,128)(2,1)S(1)}, u32[]{:S(2)}, u32[]{:S(2)}) collective-permute-start(bf16[16,4096]{1,0:T(8,128)(2,1)S(1)} %get-tuple-element.90), channel_id=1, source_target_pairs={{0,14},{1,15},{2,0},{3,1},{4,2},{5,3},{6,4},{7,5},{8,6},{9,7},{10,... | collective-permute-start | bytes 393224 | tf_op jit(solution)/shard_map/ppermute | solution.py:43
  53.1 2.4 %collective-permute-start.17 = (bf16[8,4096]{1,0:T(8,128)(2,1)S(1)}, bf16[8,4096]{1,0:T(8,128)(2,1)S(1)}, u32[]{:S(2)}, u32[]{:S(2)}) collective-permute-start(bf16[8,4096]{1,0:T(8,128)(2,1)S(1)} %slice.170), channel_id=1, source_target_pairs={{0,8},{1,9},{2,10},{3,11},{4,12},{5,13},{6,14},{7,15},{8,0},{9,1},... | collective-permute-start | bytes 196616 | tf_op jit(solution)/shard_map/ppermute | solution.py:43
  55.5 1.0 collective-permute-done.14
  56.5 0.9 collective-permute-start.16
  57.4 2.8 %collective-permute-start.18 = (bf16[8,4096]{1,0:T(8,128)(2,1)S(1)}, bf16[8,4096]{1,0:T(8,128)(2,1)S(1)}, u32[]{:S(2)}, u32[]{:S(2)}) collective-permute-start(bf16[8,4096]{1,0:T(8,128)(2,1)S(1)} %get-tuple-element.88), channel_id=1, source_target_pairs={{0,12},{1,13},{2,14},{3,15},{4,0},{5,1},{6,2},{7,3},{8,4},{9,5},{1... | collective-permute-start | bytes 196616 | tf_op jit(solution)/shard_map/ppermute | solution.py:43
  60.5 1.9 collective-permute-done.16
  63.7 19.2 %all_to_all.10 = bf16[16,2,4096]{2,1,0:T(2,128)(2,1)S(1)} all-to-all(bf16[16,2,4096]{2,1,0:T(2,128)(2,1)S(1)} %reshape.26), channel_id=1, replica_groups=mesh['ctx'=16,'exp'=16] {'exp'}, dimensions={0} | all-to-all | bytes 524288 | tf_op jit(solution)/shard_map/all_to_all | solution.py:543
  83.8 2.5 %collective-permute-start.21 = (bf16[32,4096]{1,0:T(8,128)(2,1)S(1)}, bf16[32,4096]{1,0:T(8,128)(2,1)S(1)}, u32[]{:S(2)}, u32[]{:S(2)}) collective-permute-start(bf16[32,4096]{1,0:T(8,128)(2,1)S(1)} %pad_maximum_fusion.2), channel_id=1, source_target_pairs={{0,192},{1,49},{2,194},{3,51},{4,196},{5,53},{6,198},{7,55},{8,200... | collective-permute-start | bytes 786440 | tf_op jit(solution)/shard_map/ppermute | solution.py:455
  86.4 0.7 collective-permute-start.20
  87.1 5.4 %collective-permute-done.21 = bf16[32,4096]{1,0:T(8,128)(2,1)S(1)} collective-permute-done((bf16[32,4096]{1,0:T(8,128)(2,1)S(1)}, bf16[32,4096]{1,0:T(8,128)(2,1)S(1)}, u32[]{:S(2)}, u32[]{:S(2)}) %collective-permute-start.21) | collective-permute-done | bytes 262176 | tf_op jit(solution)/shard_map/ppermute | solution.py:455
  92.5 0.9 collective-permute-done.20
  93.5 2.7 %collective-permute-done.19 = bf16[32,4096]{1,0:T(8,128)(2,1)S(1)} collective-permute-done((bf16[32,4096]{1,0:T(8,128)(2,1)S(1)}, bf16[32,4096]{1,0:T(8,128)(2,1)S(1)}, u32[]{:S(2)}, u32[]{:S(2)}) %collective-permute-start.19) | collective-permute-done | bytes 262176 | tf_op jit(solution)/shard_map/ppermute | solution.py:455
  96.4 2.7 %collective-permute-start.23 = (bf16[128,4096]{1,0:T(8,128)(2,1)S(1)}, bf16[128,4096]{1,0:T(8,128)(2,1)S(1)}, u32[]{:S(2)}, u32[]{:S(2)}) collective-permute-start(bf16[128,4096]{1,0:T(8,128)(2,1)S(1)} %join.3.after_ref), channel_id=1, source_target_pairs={{0,48},{1,193},{2,50},{3,195},{4,52},{5,197},{6,54},{7,199},{8,56}... | collective-permute-start | bytes 3145736 | tf_op jit(solution)/shard_map/ppermute | solution.py:455
  99.1 1.0 collective-permute-start.24
  100.2 3.5 %fetch.1 = (bf16[4096,512]{1,0:T(8,128)(2,1)S(1)}, bf16[512,4096]{1,0:T(8,128)(2,1)S(1)}) custom-call(bf16[128,4096]{1,0:T(8,128)(2,1)S(1)} %join.3.after_ref, bf16[4096,512]{1,0:T(8,128)(2,1)} %bitcast.16, bf16[512,4096]{1,0:T(8,128)(2,1)} %bitcast.17), custom_call_target="tpu_custom_call" | custom-call | bytes 33554432 | tf_op jit(solution)/shard_map/fetch/pallas_call | solution.py:424
  103.7 4.0 %expert.3 = (bf16[64,4096]{1,0:T(8,128)(2,1)S(1)}, bf16[64,4096]{1,0:T(8,128)(2,1)S(1)}) custom-call(bf16[64,4096]{1,0:T(8,128)(2,1)S(1)} %get-tuple-element.78.refs_0_, bf16[64,4096]{1,0:T(8,128)(2,1)S(1)} %collective-permute-done.24.refs_1_, bf16[4096,512]{1,0:T(8,128)(2,1)S(1)} %get-tuple-element.60.refs_2_.refs_4_, ...), custom_call_target="tpu_custom_call" | custom-call | flops 1073741824 | bytes 2097152 | tf_op jit(solution)/shard_map/expert/pallas_call | solution.py:400
  107.7 3.9 %collective-permute-done.22 = bf16[128,4096]{1,0:T(8,128)(2,1)S(1)} collective-permute-done((bf16[128,4096]{1,0:T(8,128)(2,1)S(1)}, bf16[128,4096]{1,0:T(8,128)(2,1)S(1)}, u32[]{:S(2)}, u32[]{:S(2)}) %collective-permute-start.22) | collective-permute-done | bytes 1048608 | tf_op jit(solution)/shard_map/ppermute | solution.py:455
  111.6 2.5 %collective-permute-start.28 = (bf16[64,4096]{1,0:T(8,128)(2,1)S(1)}, bf16[64,4096]{1,0:T(8,128)(2,1)S(1)}, u32[]{:S(2)}, u32[]{:S(2)}) collective-permute-start(bf16[64,4096]{1,0:T(8,128)(2,1)S(1)} %get-tuple-element.76), channel_id=1, source_target_pairs={{0,48},{1,193},{2,50},{3,195},{4,52},{5,197},{6,54},{7,199},{8,56}... | collective-permute-start | bytes 1572872 | tf_op jit(solution)/shard_map/ppermute | solution.py:455
  114.3 5.9 %collective-permute-done.28 = bf16[64,4096]{1,0:T(8,128)(2,1)S(1)} collective-permute-done((bf16[64,4096]{1,0:T(8,128)(2,1)S(1)}, bf16[64,4096]{1,0:T(8,128)(2,1)S(1)}, u32[]{:S(2)}, u32[]{:S(2)}) %collective-permute-start.28) | collective-permute-done | bytes 524320 | tf_op jit(solution)/shard_map/ppermute | solution.py:455
  120.2 2.7 %collective-permute-start.29 = (bf16[64,4096]{1,0:T(8,128)(2,1)S(1)}, bf16[64,4096]{1,0:T(8,128)(2,1)S(1)}, u32[]{:S(2)}, u32[]{:S(2)}) collective-permute-start(bf16[64,4096]{1,0:T(8,128)(2,1)S(1)} %collective-permute-done.28), channel_id=1, source_target_pairs={{0,1},{1,0},{2,3},{3,2},{4,5},{5,4},{6,7},{7,6},{8,9},{9,8},{10,11... | collective-permute-start | bytes 1572872 | tf_op jit(solution)/shard_map/ppermute | solution.py:43
  124.4 3.9 %expert.5 = (bf16[64,4096]{1,0:T(8,128)(2,1)S(1)}, bf16[64,4096]{1,0:T(8,128)(2,1)S(1)}) custom-call(bf16[64,4096]{1,0:T(8,128)(2,1)S(1)} %collective-permute-done.27.refs_0_, bf16[64,4096]{1,0:T(8,128)(2,1)S(1)} %collective-permute-done.29.refs_1_, bf16[4096,512]{1,0:T(8,128)(2,1)S(1)} %get-tuple-element.60.refs_2_.refs_4_, ...), custom_call_target="tpu_custom_call" | custom-call | flops 1073741824 | bytes 2097152 | tf_op jit(solution)/shard_map/expert/pallas_call | solution.py:400
  128.4 2.4 %collective-permute-start.34 = (bf16[64,4096]{1,0:T(8,128)(2,1)S(1)}, bf16[64,4096]{1,0:T(8,128)(2,1)S(1)}, u32[]{:S(2)}, u32[]{:S(2)}) collective-permute-start(bf16[64,4096]{1,0:T(8,128)(2,1)S(1)} %get-tuple-element.67), channel_id=1, source_target_pairs={{0,1},{1,0},{2,3},{3,2},{4,5},{5,4},{6,7},{7,6},{8,9},{9,8},{10,11... | collective-permute-start | bytes 1572872 | tf_op jit(solution)/shard_map/ppermute | solution.py:43
  131.4 5.2 %expert.4 = (bf16[64,4096]{1,0:T(8,128)(2,1)S(1)}, bf16[64,4096]{1,0:T(8,128)(2,1)S(1)}, bf16[64,4096]{1,0:T(8,128)(2,1)S(1)}, bf16[64,4096]{1,0:T(8,128)(2,1)S(1)}) custom-call(bf16[64,4096]{1,0:T(8,128)(2,1)S(1)} %get-tuple-element.74.refs_0_, bf16[64,4096]{1,0:T(8,128)(2,1)S(1)} %get-tuple-element.75.refs_1_, ...), custom_call_target="tpu_custom_call" | custom-call | flops 2147483648 | bytes 4194304 | tf_op jit(solution)/shard_map/expert/pallas_call | solution.py:400
  136.6 1.3 collective-permute-start.31
  138.1 1.1 collective-permute-done.30
  139.6 1.5 collective-permute-start.32
  141.0 6.5 %collective-permute-done.35 = bf16[64,4096]{1,0:T(8,128)(2,1)S(1)} collective-permute-done((bf16[64,4096]{1,0:T(8,128)(2,1)S(1)}, bf16[64,4096]{1,0:T(8,128)(2,1)S(1)}, u32[]{:S(2)}, u32[]{:S(2)}) %collective-permute-start.35) | collective-permute-done | bytes 524320 | tf_op jit(solution)/shard_map/ppermute | solution.py:455
  147.9 1.4 collective-permute-start.37
  149.2 1.5 collective-permute-done.37
  150.8 2.8 %collective-permute-done.32 = bf16[128,4096]{1,0:T(8,128)(2,1)S(1)} collective-permute-done((bf16[128,4096]{1,0:T(8,128)(2,1)S(1)}, bf16[128,4096]{1,0:T(8,128)(2,1)S(1)}, u32[]{:S(2)}, u32[]{:S(2)}) %collective-permute-start.32) | collective-permute-done | bytes 1048608 | tf_op jit(solution)/shard_map/ppermute | solution.py:455
  153.6 9.4 %collective-permute-done.36 = bf16[128,4096]{1,0:T(8,128)(2,1)S(1)} collective-permute-done((bf16[128,4096]{1,0:T(8,128)(2,1)S(1)}, bf16[128,4096]{1,0:T(8,128)(2,1)S(1)}, u32[]{:S(2)}, u32[]{:S(2)}) %collective-permute-start.36) | collective-permute-done | bytes 1048608 | tf_op jit(solution)/shard_map/ppermute | solution.py:455
  164.1 0.9 collective-permute-start.39
  165.4 3.8 %collective-permute-done.38 = bf16[32,4096]{1,0:T(8,128)(2,1)S(1)} collective-permute-done((bf16[32,4096]{1,0:T(8,128)(2,1)S(1)}, bf16[32,4096]{1,0:T(8,128)(2,1)S(1)}, u32[]{:S(2)}, u32[]{:S(2)}) %collective-permute-start.38) | collective-permute-done | bytes 262176 | tf_op jit(solution)/shard_map/ppermute | solution.py:455
  169.2 1.8 collective-permute-done.39
  171.0 3.0 %collective-permute-done.40 = bf16[32,4096]{1,0:T(8,128)(2,1)S(1)} collective-permute-done((bf16[32,4096]{1,0:T(8,128)(2,1)S(1)}, bf16[32,4096]{1,0:T(8,128)(2,1)S(1)}, u32[]{:S(2)}, u32[]{:S(2)}) %collective-permute-start.40) | collective-permute-done | bytes 262176 | tf_op jit(solution)/shard_map/ppermute | solution.py:455
  174.2 1.0 copy.47
  175.2 6.9 %all-to-all-start.1 = ((bf16[16,2,4096]{2,1,0:T(2,128)(2,1)}), bf16[16,2,4096]{2,1,0:T(2,128)(2,1)S(1)}, u32[]{:S(2)}, u32[]{:S(2)}) async-start(bf16[16,2,4096]{2,1,0:T(2,128)(2,1)} %copy.47), calls=%async_computation.1 | async-start | bytes 524288 | tf_op jit(solution)/shard_map/all_to_all | solution.py:546
  182.2 11.7 %all-to-all-done.1 = bf16[16,2,4096]{2,1,0:T(2,128)(2,1)S(1)} async-done(((bf16[16,2,4096]{2,1,0:T(2,128)(2,1)}), bf16[16,2,4096]{2,1,0:T(2,128)(2,1)S(1)}, u32[]{:S(2)}, u32[]{:S(2)}) %all-to-all-start.1) | async-done | bytes 262176 | tf_op jit(solution)/shard_map/all_to_all | solution.py:546
  193.9 0.9 fusion
  (87 shorter events, 9.7 us)
Async XLA Ops:
  0.7 5.4 %collective-permute-start = (bf16[3,512]{1,0:T(4,128)(2,1)S(1)}, bf16[3,512]{1,0:T(4,128)(2,1)S(1)}, u32[]{:S(2)}, u32[]{:S(2)}) collective-permute-start(bf16[3,512]{1,0:T(4,128)(2,1)S(1)} %slice.124), channel_id=1, source_target_pairs={{0,16},{16,32},{32,48},{48,64},{64,80},{80,96},{96,112},{112,128},... | collective-permute-start | bytes 9224 | tf_op jit(solution)/shard_map/ppermute | solution.py:25
  6.3 2.7 %collective-permute-start.1 = (f32[32,128]{1,0:T(8,128)S(1)}, f32[32,128]{1,0:T(8,128)S(1)}, u32[]{:S(2)}, u32[]{:S(2)}) collective-permute-start(f32[32,128]{1,0:T(8,128)S(1)} %get-tuple-element.41), channel_id=1, source_target_pairs={{0,1},{1,0},{2,3},{3,2},{4,5},{5,4},{6,7},{7,6},{8,9},{9,8},{10,11... | collective-permute-start | bytes 49160 | tf_op jit(solution)/shard_map/ppermute | solution.py:43
  7.2 2.8 %collective-permute-start.2 = (f32[32,128]{1,0:T(8,128)S(1)}, f32[32,128]{1,0:T(8,128)S(1)}, u32[]{:S(2)}, u32[]{:S(2)}) collective-permute-start(f32[32,128]{1,0:T(8,128)S(1)} %get-tuple-element.41), channel_id=1, source_target_pairs={{0,2},{1,3},{2,0},{3,1},{4,6},{5,7},{6,4},{7,5},{8,10},{9,11},{10,... | collective-permute-start | bytes 49160 | tf_op jit(solution)/shard_map/ppermute | solution.py:43
  8.9 3.2 %collective-permute-start.3 = (f32[32,128]{1,0:T(8,128)S(1)}, f32[32,128]{1,0:T(8,128)S(1)}, u32[]{:S(2)}, u32[]{:S(2)}) collective-permute-start(f32[32,128]{1,0:T(8,128)S(1)} %get-tuple-element.41), channel_id=1, source_target_pairs={{0,3},{1,2},{2,1},{3,0},{4,7},{5,6},{6,5},{7,4},{8,11},{9,10},{10,... | collective-permute-start | bytes 49160 | tf_op jit(solution)/shard_map/ppermute | solution.py:43
  12.1 9.6 %collective-permute-start.4 = (f32[32,128]{1,0:T(8,128)S(1)}, f32[32,128]{1,0:T(8,128)S(1)}, u32[]{:S(2)}, u32[]{:S(2)}) collective-permute-start(f32[32,128]{1,0:T(8,128)S(1)} %add_add_fusion.a_ref), channel_id=1, source_target_pairs={{0,4},{1,5},{2,6},{3,7},{4,8},{5,9},{6,10},{7,11},{8,12},{9,13},{1... | collective-permute-start | bytes 49160 | tf_op jit(solution)/shard_map/ppermute | solution.py:43
  15.1 6.6 %collective-permute-start.5 = (f32[32,128]{1,0:T(8,128)S(1)}, f32[32,128]{1,0:T(8,128)S(1)}, u32[]{:S(2)}, u32[]{:S(2)}) collective-permute-start(f32[32,128]{1,0:T(8,128)S(1)} %add_add_fusion.a_ref), channel_id=1, source_target_pairs={{0,8},{1,9},{2,10},{3,11},{4,12},{5,13},{6,14},{7,15},{8,0},{9,1},... | collective-permute-start | bytes 49160 | tf_op jit(solution)/shard_map/ppermute | solution.py:43
  19.3 3.7 %collective-permute-start.6 = (f32[32,128]{1,0:T(8,128)S(1)}, f32[32,128]{1,0:T(8,128)S(1)}, u32[]{:S(2)}, u32[]{:S(2)}) collective-permute-start(f32[32,128]{1,0:T(8,128)S(1)} %add_add_fusion.a_ref), channel_id=1, source_target_pairs={{0,12},{1,13},{2,14},{3,15},{4,0},{5,1},{6,2},{7,3},{8,4},{9,5},{1... | collective-permute-start | bytes 49160 | tf_op jit(solution)/shard_map/ppermute | solution.py:43
  24.1 5.7 %collective-permute-start.7 = (bf16[32,512]{1,0:T(8,128)(2,1)S(1)}, bf16[32,512]{1,0:T(8,128)(2,1)S(1)}, u32[]{:S(2)}, u32[]{:S(2)}) collective-permute-start(bf16[32,512]{1,0:T(8,128)(2,1)S(1)} %get-tuple-element.44.a_ref), channel_id=1, source_target_pairs={{0,16},{16,32},{32,48},{48,0},{64,80},{80,96},{96,112},{112,64},{1... | collective-permute-start | bytes 98312 | tf_op jit(solution)/shard_map/ppermute | solution.py:34
  26.2 4.3 %collective-permute-start.8 = (bf16[32,512]{1,0:T(8,128)(2,1)S(1)}, bf16[32,512]{1,0:T(8,128)(2,1)S(1)}, u32[]{:S(2)}, u32[]{:S(2)}) collective-permute-start(bf16[32,512]{1,0:T(8,128)(2,1)S(1)} %get-tuple-element.44.a_ref), channel_id=1, source_target_pairs={{0,32},{16,48},{32,0},{48,16},{64,96},{80,112},{96,64},{112,80},{1... | collective-permute-start | bytes 98312 | tf_op jit(solution)/shard_map/ppermute | solution.py:34
  28.8 2.8 %collective-permute-start.9 = (bf16[32,512]{1,0:T(8,128)(2,1)S(1)}, bf16[32,512]{1,0:T(8,128)(2,1)S(1)}, u32[]{:S(2)}, u32[]{:S(2)}) collective-permute-start(bf16[32,512]{1,0:T(8,128)(2,1)S(1)} %get-tuple-element.44.a_ref), channel_id=1, source_target_pairs={{0,48},{16,0},{32,16},{48,32},{64,112},{80,64},{96,80},{112,96},{1... | collective-permute-start | bytes 98312 | tf_op jit(solution)/shard_map/ppermute | solution.py:34
  31.7 5.2 %collective-permute-start.10 = (bf16[32,512]{1,0:T(8,128)(2,1)S(1)}, bf16[32,512]{1,0:T(8,128)(2,1)S(1)}, u32[]{:S(2)}, u32[]{:S(2)}) collective-permute-start(bf16[32,512]{1,0:T(8,128)(2,1)S(1)} %get-tuple-element.45.refs_0_), channel_id=1, source_target_pairs={{0,64},{16,80},{32,96},{48,112},{64,128},{80,144},{96,160},{112,17... | collective-permute-start | bytes 98312 | tf_op jit(solution)/shard_map/ppermute | solution.py:34
  33.3 4.3 %collective-permute-start.11 = (bf16[32,512]{1,0:T(8,128)(2,1)S(1)}, bf16[32,512]{1,0:T(8,128)(2,1)S(1)}, u32[]{:S(2)}, u32[]{:S(2)}) collective-permute-start(bf16[32,512]{1,0:T(8,128)(2,1)S(1)} %get-tuple-element.45.refs_0_), channel_id=1, source_target_pairs={{0,128},{16,144},{32,160},{48,176},{64,192},{80,208},{96,224},{112... | collective-permute-start | bytes 98312 | tf_op jit(solution)/shard_map/ppermute | solution.py:34
  35.8 2.8 %collective-permute-start.12 = (bf16[32,512]{1,0:T(8,128)(2,1)S(1)}, bf16[32,512]{1,0:T(8,128)(2,1)S(1)}, u32[]{:S(2)}, u32[]{:S(2)}) collective-permute-start(bf16[32,512]{1,0:T(8,128)(2,1)S(1)} %get-tuple-element.45.refs_0_), channel_id=1, source_target_pairs={{0,192},{16,208},{32,224},{48,240},{64,0},{80,16},{96,32},{112,48}... | collective-permute-start | bytes 98312 | tf_op jit(solution)/shard_map/ppermute | solution.py:34
  38.6 9.4 %copy-start.2 = (s32[8,2]{0,1:T(2,128)S(1)}, s32[8,2]{0,1:T(2,128)}, u32[]{:S(2)}) copy-start(s32[8,2]{0,1:T(2,128)} %param.26) | copy-start | bytes 196
  42.9 20.2 %copy-start = (bf16[8,4096]{1,0:T(8,128)(2,1)S(1)}, bf16[8,4096]{1,0:T(8,128)(2,1)}, u32[]{:S(2)}) copy-start(bf16[8,4096]{1,0:T(8,128)(2,1)} %param.24) | copy-start | bytes 196612
  42.9 20.4 %copy-start.1 = (f32[4096]{0:T(1024)S(1)}, f32[4096]{0:T(1024)}, u32[]{:S(2)}) copy-start(f32[4096]{0:T(1024)} %param.25) | copy-start | bytes 49156
  42.9 6.6 %collective-permute-start.13 = (bf16[64,4096]{1,0:T(8,128)(2,1)S(1)}, bf16[64,4096]{1,0:T(8,128)(2,1)S(1)}, u32[]{:S(2)}, u32[]{:S(2)}) collective-permute-start(bf16[64,4096]{1,0:T(8,128)(2,1)S(1)} %get-tuple-element.52), channel_id=1, source_target_pairs={{0,1},{1,0},{2,3},{3,2},{4,5},{5,4},{6,7},{7,6},{8,9},{9,8},{10,11... | collective-permute-start | bytes 1572872 | tf_op jit(solution)/shard_map/ppermute | solution.py:43
  49.7 6.8 %collective-permute-start.14 = (bf16[16,4096]{1,0:T(8,128)(2,1)S(1)}, bf16[16,4096]{1,0:T(8,128)(2,1)S(1)}, u32[]{:S(2)}, u32[]{:S(2)}) collective-permute-start(bf16[16,4096]{1,0:T(8,128)(2,1)S(1)} %get-tuple-element.89), channel_id=1, source_target_pairs={{0,2},{1,3},{2,4},{3,5},{4,6},{5,7},{6,8},{7,9},{8,10},{9,11},{10,... | collective-permute-start | bytes 393224 | tf_op jit(solution)/shard_map/ppermute | solution.py:43
  50.5 6.0 %collective-permute-start.15 = (bf16[16,4096]{1,0:T(8,128)(2,1)S(1)}, bf16[16,4096]{1,0:T(8,128)(2,1)S(1)}, u32[]{:S(2)}, u32[]{:S(2)}) collective-permute-start(bf16[16,4096]{1,0:T(8,128)(2,1)S(1)} %get-tuple-element.90), channel_id=1, source_target_pairs={{0,14},{1,15},{2,0},{3,1},{4,2},{5,3},{6,4},{7,5},{8,6},{9,7},{10,... | collective-permute-start | bytes 393224 | tf_op jit(solution)/shard_map/ppermute | solution.py:43
  53.1 7.4 %collective-permute-start.17 = (bf16[8,4096]{1,0:T(8,128)(2,1)S(1)}, bf16[8,4096]{1,0:T(8,128)(2,1)S(1)}, u32[]{:S(2)}, u32[]{:S(2)}) collective-permute-start(bf16[8,4096]{1,0:T(8,128)(2,1)S(1)} %slice.170), channel_id=1, source_target_pairs={{0,8},{1,9},{2,10},{3,11},{4,12},{5,13},{6,14},{7,15},{8,0},{9,1},... | collective-permute-start | bytes 196616 | tf_op jit(solution)/shard_map/ppermute | solution.py:43
  56.5 5.9 %collective-permute-start.16 = (bf16[8,4096]{1,0:T(8,128)(2,1)S(1)}, bf16[8,4096]{1,0:T(8,128)(2,1)S(1)}, u32[]{:S(2)}, u32[]{:S(2)}) collective-permute-start(bf16[8,4096]{1,0:T(8,128)(2,1)S(1)} %get-tuple-element.87), channel_id=1, source_target_pairs={{0,4},{1,5},{2,6},{3,7},{4,8},{5,9},{6,10},{7,11},{8,12},{9,13},{1... | collective-permute-start | bytes 196616 | tf_op jit(solution)/shard_map/ppermute | solution.py:43
  57.4 5.7 %collective-permute-start.18 = (bf16[8,4096]{1,0:T(8,128)(2,1)S(1)}, bf16[8,4096]{1,0:T(8,128)(2,1)S(1)}, u32[]{:S(2)}, u32[]{:S(2)}) collective-permute-start(bf16[8,4096]{1,0:T(8,128)(2,1)S(1)} %get-tuple-element.88), channel_id=1, source_target_pairs={{0,12},{1,13},{2,14},{3,15},{4,0},{5,1},{6,2},{7,3},{8,4},{9,5},{1... | collective-permute-start | bytes 196616 | tf_op jit(solution)/shard_map/ppermute | solution.py:43
  83.8 8.7 %collective-permute-start.21 = (bf16[32,4096]{1,0:T(8,128)(2,1)S(1)}, bf16[32,4096]{1,0:T(8,128)(2,1)S(1)}, u32[]{:S(2)}, u32[]{:S(2)}) collective-permute-start(bf16[32,4096]{1,0:T(8,128)(2,1)S(1)} %pad_maximum_fusion.2), channel_id=1, source_target_pairs={{0,192},{1,49},{2,194},{3,51},{4,196},{5,53},{6,198},{7,55},{8,200... | collective-permute-start | bytes 786440 | tf_op jit(solution)/shard_map/ppermute | solution.py:455
  86.4 7.1 %collective-permute-start.20 = (bf16[32,4096]{1,0:T(8,128)(2,1)S(1)}, bf16[32,4096]{1,0:T(8,128)(2,1)S(1)}, u32[]{:S(2)}, u32[]{:S(2)}) collective-permute-start(bf16[32,4096]{1,0:T(8,128)(2,1)S(1)} %pad_maximum_fusion.2), channel_id=1, source_target_pairs={{0,128},{1,33},{2,130},{3,35},{4,132},{5,37},{6,134},{7,39},{8,136... | collective-permute-start | bytes 786440 | tf_op jit(solution)/shard_map/ppermute | solution.py:455
  87.1 9.1 %collective-permute-start.19 = (bf16[32,4096]{1,0:T(8,128)(2,1)S(1)}, bf16[32,4096]{1,0:T(8,128)(2,1)S(1)}, u32[]{:S(2)}, u32[]{:S(2)}) collective-permute-start(bf16[32,4096]{1,0:T(8,128)(2,1)S(1)} %pad_maximum_fusion.2), channel_id=1, source_target_pairs={{0,64},{1,17},{2,66},{3,19},{4,68},{5,21},{6,70},{7,23},{8,72},{9,... | collective-permute-start | bytes 786440 | tf_op jit(solution)/shard_map/ppermute | solution.py:455
  96.3 15.2 %collective-permute-start.22 = (bf16[128,4096]{1,0:T(8,128)(2,1)S(1)}, bf16[128,4096]{1,0:T(8,128)(2,1)S(1)}, u32[]{:S(2)}, u32[]{:S(2)}) collective-permute-start(bf16[128,4096]{1,0:T(8,128)(2,1)S(1)} %join.3.after_ref), channel_id=1, source_target_pairs={{0,16},{1,65},{2,18},{3,67},{4,20},{5,69},{6,22},{7,71},{8,24},{9,... | collective-permute-start | bytes 3145736 | tf_op jit(solution)/shard_map/ppermute | solution.py:455
  96.4 15.1 %collective-permute-start.23 = (bf16[128,4096]{1,0:T(8,128)(2,1)S(1)}, bf16[128,4096]{1,0:T(8,128)(2,1)S(1)}, u32[]{:S(2)}, u32[]{:S(2)}) collective-permute-start(bf16[128,4096]{1,0:T(8,128)(2,1)S(1)} %join.3.after_ref), channel_id=1, source_target_pairs={{0,48},{1,193},{2,50},{3,195},{4,52},{5,197},{6,54},{7,199},{8,56}... | collective-permute-start | bytes 3145736 | tf_op jit(solution)/shard_map/ppermute | solution.py:455
  99.1 4.5 %collective-permute-start.24 = (bf16[64,4096]{1,0:T(8,128)(2,1)S(1)}, bf16[64,4096]{1,0:T(8,128)(2,1)S(1)}, u32[]{:S(2)}, u32[]{:S(2)}) collective-permute-start(bf16[64,4096]{1,0:T(8,128)(2,1)S(1)} %get-tuple-element.77), channel_id=1, source_target_pairs={{0,1},{1,0},{2,3},{3,2},{4,5},{5,4},{6,7},{7,6},{8,9},{9,8},{10,11... | collective-permute-start | bytes 1572872 | tf_op jit(solution)/shard_map/ppermute | solution.py:43
  111.6 8.6 %collective-permute-start.28 = (bf16[64,4096]{1,0:T(8,128)(2,1)S(1)}, bf16[64,4096]{1,0:T(8,128)(2,1)S(1)}, u32[]{:S(2)}, u32[]{:S(2)}) collective-permute-start(bf16[64,4096]{1,0:T(8,128)(2,1)S(1)} %get-tuple-element.76), channel_id=1, source_target_pairs={{0,48},{1,193},{2,50},{3,195},{4,52},{5,197},{6,54},{7,199},{8,56}... | collective-permute-start | bytes 1572872 | tf_op jit(solution)/shard_map/ppermute | solution.py:455
  114.2 9.6 %collective-permute-start.27 = (bf16[64,4096]{1,0:T(8,128)(2,1)S(1)}, bf16[64,4096]{1,0:T(8,128)(2,1)S(1)}, u32[]{:S(2)}, u32[]{:S(2)}) collective-permute-start(bf16[64,4096]{1,0:T(8,128)(2,1)S(1)} %get-tuple-element.74.refs_0_), channel_id=1, source_target_pairs={{0,16},{1,65},{2,18},{3,67},{4,20},{5,69},{6,22},{7,71},{8,24},{9,... | collective-permute-start | bytes 1572872 | tf_op jit(solution)/shard_map/ppermute | solution.py:455
  120.2 4.2 %collective-permute-start.29 = (bf16[64,4096]{1,0:T(8,128)(2,1)S(1)}, bf16[64,4096]{1,0:T(8,128)(2,1)S(1)}, u32[]{:S(2)}, u32[]{:S(2)}) collective-permute-start(bf16[64,4096]{1,0:T(8,128)(2,1)S(1)} %collective-permute-done.28), channel_id=1, source_target_pairs={{0,1},{1,0},{2,3},{3,2},{4,5},{5,4},{6,7},{7,6},{8,9},{9,8},{10,11... | collective-permute-start | bytes 1572872 | tf_op jit(solution)/shard_map/ppermute | solution.py:43
  122.9 8.5 %collective-permute-start.25 = (bf16[64,4096]{1,0:T(8,128)(2,1)S(1)}, bf16[64,4096]{1,0:T(8,128)(2,1)S(1)}, u32[]{:S(2)}, u32[]{:S(2)}) collective-permute-start(bf16[64,4096]{1,0:T(8,128)(2,1)S(1)} %get-tuple-element.73), channel_id=1, source_target_pairs={{0,1},{1,0},{2,3},{3,2},{4,5},{5,4},{6,7},{7,6},{8,9},{9,8},{10,11... | collective-permute-start | bytes 1572872 | tf_op jit(solution)/shard_map/ppermute | solution.py:43
  122.9 8.5 %collective-permute-start.26 = (bf16[64,4096]{1,0:T(8,128)(2,1)S(1)}, bf16[64,4096]{1,0:T(8,128)(2,1)S(1)}, u32[]{:S(2)}, u32[]{:S(2)}) collective-permute-start(bf16[64,4096]{1,0:T(8,128)(2,1)S(1)} %get-tuple-element.76), channel_id=1, source_target_pairs={{0,1},{1,0},{2,3},{3,2},{4,5},{5,4},{6,7},{7,6},{8,9},{9,8},{10,11... | collective-permute-start | bytes 1572872 | tf_op jit(solution)/shard_map/ppermute | solution.py:43
  128.4 9.7 %collective-permute-start.34 = (bf16[64,4096]{1,0:T(8,128)(2,1)S(1)}, bf16[64,4096]{1,0:T(8,128)(2,1)S(1)}, u32[]{:S(2)}, u32[]{:S(2)}) collective-permute-start(bf16[64,4096]{1,0:T(8,128)(2,1)S(1)} %get-tuple-element.67), channel_id=1, source_target_pairs={{0,1},{1,0},{2,3},{3,2},{4,5},{5,4},{6,7},{7,6},{8,9},{9,8},{10,11... | collective-permute-start | bytes 1572872 | tf_op jit(solution)/shard_map/ppermute | solution.py:43
  130.8 8.3 %collective-permute-start.30 = (bf16[64,4096]{1,0:T(8,128)(2,1)S(1)}, bf16[64,4096]{1,0:T(8,128)(2,1)S(1)}, u32[]{:S(2)}, u32[]{:S(2)}) collective-permute-start(bf16[64,4096]{1,0:T(8,128)(2,1)S(1)} %get-tuple-element.63), channel_id=1, source_target_pairs={{0,48},{1,193},{2,50},{3,195},{4,52},{5,197},{6,54},{7,199},{8,56}... | collective-permute-start | bytes 1572872 | tf_op jit(solution)/shard_map/ppermute | solution.py:455
  136.6 2.9 %collective-permute-start.31 = (bf16[64,4096]{1,0:T(8,128)(2,1)S(1)}, bf16[64,4096]{1,0:T(8,128)(2,1)S(1)}, u32[]{:S(2)}, u32[]{:S(2)}) collective-permute-start(bf16[64,4096]{1,0:T(8,128)(2,1)S(1)} %get-tuple-element.64), channel_id=1, source_target_pairs={{0,1},{1,0},{2,3},{3,2},{4,5},{5,4},{6,7},{7,6},{8,9},{9,8},{10,11... | collective-permute-start | bytes 1572872 | tf_op jit(solution)/shard_map/ppermute | solution.py:43
  137.9 3.1 %collective-permute-start.33 = (bf16[64,4096]{1,0:T(8,128)(2,1)S(1)}, bf16[64,4096]{1,0:T(8,128)(2,1)S(1)}, u32[]{:S(2)}, u32[]{:S(2)}) collective-permute-start(bf16[64,4096]{1,0:T(8,128)(2,1)S(1)} %get-tuple-element.66), channel_id=1, source_target_pairs={{0,1},{1,0},{2,3},{3,2},{4,5},{5,4},{6,7},{7,6},{8,9},{9,8},{10,11... | collective-permute-start | bytes 1572872 | tf_op jit(solution)/shard_map/ppermute | solution.py:43
  138.0 9.5 %collective-permute-start.35 = (bf16[64,4096]{1,0:T(8,128)(2,1)S(1)}, bf16[64,4096]{1,0:T(8,128)(2,1)S(1)}, u32[]{:S(2)}, u32[]{:S(2)}) collective-permute-start(bf16[64,4096]{1,0:T(8,128)(2,1)S(1)} %collective-permute-done.34), channel_id=1, source_target_pairs={{0,16},{1,65},{2,18},{3,67},{4,20},{5,69},{6,22},{7,71},{8,24},{9,... | collective-permute-start | bytes 1572872 | tf_op jit(solution)/shard_map/ppermute | solution.py:455
  139.6 14.0 %collective-permute-start.32 = (bf16[128,4096]{1,0:T(8,128)(2,1)S(1)}, bf16[128,4096]{1,0:T(8,128)(2,1)S(1)}, u32[]{:S(2)}, u32[]{:S(2)}) collective-permute-start(bf16[128,4096]{1,0:T(8,128)(2,1)S(1)} %pad_maximum_fusion), channel_id=1, source_target_pairs={{0,48},{1,193},{2,50},{3,195},{4,52},{5,197},{6,54},{7,199},{8,56}... | collective-permute-start | bytes 3145736 | tf_op jit(solution)/shard_map/ppermute | solution.py:455
  147.8 15.2 %collective-permute-start.36 = (bf16[128,4096]{1,0:T(8,128)(2,1)S(1)}, bf16[128,4096]{1,0:T(8,128)(2,1)S(1)}, u32[]{:S(2)}, u32[]{:S(2)}) collective-permute-start(bf16[128,4096]{1,0:T(8,128)(2,1)S(1)} %pad_maximum_fusion.1), channel_id=1, source_target_pairs={{0,16},{1,65},{2,18},{3,67},{4,20},{5,69},{6,22},{7,71},{8,24},{9,... | collective-permute-start | bytes 3145736 | tf_op jit(solution)/shard_map/ppermute | solution.py:455
  147.9 2.9 %collective-permute-start.37 = (bf16[64,4096]{1,0:T(8,128)(2,1)S(1)}, bf16[64,4096]{1,0:T(8,128)(2,1)S(1)}, u32[]{:S(2)}, u32[]{:S(2)}) collective-permute-start(bf16[64,4096]{1,0:T(8,128)(2,1)S(1)} %get-tuple-element.68), channel_id=1, source_target_pairs={{0,1},{1,0},{2,3},{3,2},{4,5},{5,4},{6,7},{7,6},{8,9},{9,8},{10,11... | collective-permute-start | bytes 1572872 | tf_op jit(solution)/shard_map/ppermute | solution.py:43
  163.6 5.6 %collective-permute-start.38 = (bf16[32,4096]{1,0:T(8,128)(2,1)S(1)}, bf16[32,4096]{1,0:T(8,128)(2,1)S(1)}, u32[]{:S(2)}, u32[]{:S(2)}) collective-permute-start(bf16[32,4096]{1,0:T(8,128)(2,1)S(1)} %pad_maximum_fusion.3), channel_id=1, source_target_pairs={{0,192},{1,49},{2,194},{3,51},{4,196},{5,53},{6,198},{7,55},{8,200... | collective-permute-start | bytes 786440 | tf_op jit(solution)/shard_map/ppermute | solution.py:455
  164.1 18.0 %copy-start.3 = (s32[8,2]{0,1:T(2,128)S(1)}, s32[8,2]{0,1:T(2,128)}, u32[]{:S(2)}) copy-start(s32[8,2]{0,1:T(2,128)} %param.27) | copy-start | bytes 196
  164.1 6.9 %collective-permute-start.39 = (bf16[32,4096]{1,0:T(8,128)(2,1)S(1)}, bf16[32,4096]{1,0:T(8,128)(2,1)S(1)}, u32[]{:S(2)}, u32[]{:S(2)}) collective-permute-start(bf16[32,4096]{1,0:T(8,128)(2,1)S(1)} %pad_maximum_fusion.4), channel_id=1, source_target_pairs={{0,128},{1,33},{2,130},{3,35},{4,132},{5,37},{6,134},{7,39},{8,136... | collective-permute-start | bytes 786440 | tf_op jit(solution)/shard_map/ppermute | solution.py:455
  165.0 9.0 %collective-permute-start.40 = (bf16[32,4096]{1,0:T(8,128)(2,1)S(1)}, bf16[32,4096]{1,0:T(8,128)(2,1)S(1)}, u32[]{:S(2)}, u32[]{:S(2)}) collective-permute-start(bf16[32,4096]{1,0:T(8,128)(2,1)S(1)} %pad_maximum_fusion.5), channel_id=1, source_target_pairs={{0,64},{1,17},{2,66},{3,19},{4,68},{5,21},{6,70},{7,23},{8,72},{9,... | collective-permute-start | bytes 786440 | tf_op jit(solution)/shard_map/ppermute | solution.py:455
  175.2 18.7 %all-to-all-start.1 = ((bf16[16,2,4096]{2,1,0:T(2,128)(2,1)}), bf16[16,2,4096]{2,1,0:T(2,128)(2,1)S(1)}, u32[]{:S(2)}, u32[]{:S(2)}) async-start(bf16[16,2,4096]{2,1,0:T(2,128)(2,1)} %copy.47), calls=%async_computation.1 | async-start | bytes 524288 | tf_op jit(solution)/shard_map/all_to_all | solution.py:546
where the time goes:
time: 195 us
  waiting for transfers between devices  74.2 us (38%)
  starting transfers between devices  70.5 us (36%)
  Pallas kernels  23.7 us (12%)
  blocking collectives  19.2 us (10%)
  local copies, waits for them, and re-layouts  3.6 us (2%)
  other arithmetic  1.97 us (1%)
    ppermute x14, waiting for transfers between devices, along_side(): return lax.ppermute(array, ('ctx', 'exp'), pairs)  47.7 us
    ppermute x20, starting transfers between devices, along_depth(): return lax.ppermute(array, 'exp', pairs)  36.2 us
    all_to_all x1, blocking collectives, shards(): lax.all_to_all(outgoing, 'exp', split_axis=0, concat_axis=0, tiled=True)  19.2 us
    pallas_call x3, Pallas kernels, expert(): pl.pallas_call(functools.partial(expert_kernel, len(pieces)), out_shape=t...  13.1 us
    ppermute x14, starting transfers between devices, along_side(): return lax.ppermute(array, ('ctx', 'exp'), pairs)  12.5 us
    all_to_all x1, waiting for transfers between devices, shards(): lax.all_to_all(expert_out, 'exp', split_axis=0, concat_axis=0, tiled=True)  11.7 us
    ppermute x20, waiting for transfers between devices, along_depth(): return lax.ppermute(array, 'exp', pairs)  11.5 us
    ppermute x6, starting transfers between devices, along_plane(): return lax.ppermute(array, 'ctx', pairs)  11 us
  transfers between devices with their start and end apart: 42, of which 29 were waited for; matrix products, arithmetic and copies ran while one was open for 1% of the time, Pallas kernels for 9%

commit v1 on v0

--- a/solution.py
+++ b/solution.py
@@ -462,23 +462,26 @@
     visits = [base] + [along_side(base, 0, k) for k in steps]
     group = join([v[:size] for v in visits] + [v[size:] for v in visits])
     half = group.shape[0] // 2
-    after, before = along_side(group, 1, 1), along_side(group, 1, -1)
+    before_theirs = along_side(group[half:], 1, -1)
+    after, before_mine = along_side(group, 1, 1), along_side(group[:half], 1, -1)
     up, down = fetch(group, up, down)
     own_mine, own_swapped = expert([group[:half], swap(group[half:])], up, down)
-    after, before, up, down, own_mine, own_swapped = lax.optimization_barrier(
-        (after, before, up, down, own_mine, own_swapped)
-    )
-    far_mine = along_side(after[:half], 1, 1)
-    far_theirs = along_side(before[half:], 1, -1)
-    close = [after[:half], before[:half], swap(after[half:]), swap(before[half:])]
-    far_mine, far_swapped = expert([far_mine, swap(far_theirs)], up, down)
-    passed = along_side(far_mine, 1, -1), along_side(swap(far_swapped), 1, 1)
+    after, before_mine, up, down, own_mine, own_swapped = lax.optimization_barrier(
+        (after, before_mine, up, down, own_mine, own_swapped)
+    )
+    before_swapped = swap(before_theirs)
+    far_mine, far_swapped = along_side(after[:half], 1, 1), along_side(before_swapped, 0, -1)
+    close = [after[:half], before_mine, swap(after[half:]), before_swapped]
+    far_mine, far_swapped = expert([far_mine, far_swapped], up, down)
+    passed_mine, passed_swapped = along_side(far_mine, 1, -1), along_side(far_swapped, 0, 1)
+    passed_mine, passed_swapped = lax.optimization_barrier((passed_mine, passed_swapped))
     after_mine, before_mine, after_swapped, before_swapped = expert(close, up, down)
-    own_theirs, after_theirs, before_theirs = swap(own_swapped), swap(after_swapped), swap(before_swapped)
-    one = along_side(jnp.concatenate([added(after_mine, passed[0]), after_theirs]), 1, -1)
-    three = along_side(jnp.concatenate([before_mine, added(before_theirs, passed[1])]), 1, 1)
-    total_mine = split(added(own_mine, one[:half], three[:half]), 4)
-    total_theirs = split(added(own_theirs, one[half:], three[half:]), 4)
+    own_theirs, after_theirs = swap(own_swapped), swap(after_swapped)
+    before_theirs = swap(added(before_swapped, passed_swapped))
+    one = along_side(jnp.concatenate([added(after_mine, passed_mine), after_theirs]), 1, -1)
+    three_mine, three_theirs = along_side(before_mine, 1, 1), along_side(before_theirs, 1, 1)
+    total_mine = split(added(own_mine, one[:half], three_mine), 4)
+    total_theirs = split(added(own_theirs, one[half:], three_theirs), 4)
     blocks = [jnp.concatenate([m, t]) for m, t in zip(total_mine, total_theirs)]
     return added(blocks[0], *[along_side(blocks[k], 0, -k) for k in steps])
 

time: 195 us -> 188 us (0.964)
  waiting for transfers between devices: 74.2 us -> 61.2 us
  starting transfers between devices: 70.5 us -> 77.4 us
    ppermute x14 -> x16, waiting for transfers between devices: 47.7 us -> 33.4 us  [along_side(): return lax.ppermute(array, ('ctx', 'exp'), pairs)]
    ppermute x14 -> x16, starting transfers between devices: 12.5 us -> 19.4 us  [along_side(): return lax.ppermute(array, ('ctx', 'exp'), pairs)]
    ppermute x20 -> x18, starting transfers between devices: 36.2 us -> 37.6 us  [along_depth(): return lax.ppermute(array, 'exp', pairs)]
    ppermute x20 -> x18, waiting for transfers between devices: 11.5 us -> 12.7 us  [along_depth(): return lax.ppermute(array, 'exp', pairs)]
  transfers between devices with their start and end apart: 42 -> 42, of which waited for: 29 -> 21; matrix products, arithmetic and copies ran while one was open for 1% -> 1% of each run, Pallas kernels for 9% -> 10%
where the time goes in v1:
time: 188 us
  starting transfers between devices  77.4 us (41%)
  waiting for transfers between devices  61.2 us (33%)
  Pallas kernels  23.7 us (13%)
  blocking collectives  18.5 us (10%)
  local copies, waits for them, and re-layouts  3.53 us (2%)
    ppermute x18, starting transfers between devices, along_depth(): return lax.ppermute(array, 'exp', pairs)  37.6 us
    ppermute x16, waiting for transfers between devices, along_side(): return lax.ppermute(array, ('ctx', 'exp'), pairs)  33.4 us
    ppermute x16, starting transfers between devices, along_side(): return lax.ppermute(array, ('ctx', 'exp'), pairs)  19.4 us
    all_to_all x1, blocking collectives, shards(): lax.all_to_all(outgoing, 'exp', split_axis=0, concat_axis=0, tiled=True)  18.5 us
    pallas_call x3, Pallas kernels, expert(): pl.pallas_call(functools.partial(expert_kernel, len(pieces)), out_shape=t...  13.1 us
    ppermute x18, waiting for transfers between devices, along_depth(): return lax.ppermute(array, 'exp', pairs)  12.7 us
    all_to_all x1, waiting for transfers between devices, shards(): lax.all_to_all(expert_out, 'exp', split_axis=0, concat_axis=0, tiled=True)  11.7 us
    ppermute x6, starting transfers between devices, along_plane(): return lax.ppermute(array, 'ctx', pairs)  10.6 us
  transfers between devices with their start and end apart: 42, of which 21 were waited for; matrix products, arithmetic and copies ran while one was open for 1% of the time, Pallas kernels for 10%

profile of v1, /device:TPU:1, one launch (start us, length us, event | category | flops | bytes accessed | tf_op | source)
XLA Modules:
  0.0 187.8 jit_solution(969295356099423944)
XLA Ops:
  0.0 0.7 slice.113
  0.7 4.0 %collective-permute-start = (bf16[3,512]{1,0:T(4,128)(2,1)S(1)}, bf16[3,512]{1,0:T(4,128)(2,1)S(1)}, u32[]{:S(2)}, u32[]{:S(2)}) collective-permute-start(bf16[3,512]{1,0:T(4,128)(2,1)S(1)} %slice.113), channel_id=1, source_target_pairs={{0,16},{16,32},{32,48},{48,64},{64,80},{80,96},{96,112},{112,128},... | collective-permute-start | bytes 9224 | tf_op jit(solution)/shard_map/ppermute | solution.py:25
  4.7 1.3 stage.1
  6.3 2.5 %collective-permute-start.3 = (f32[32,128]{1,0:T(8,128)S(1)}, f32[32,128]{1,0:T(8,128)S(1)}, u32[]{:S(2)}, u32[]{:S(2)}) collective-permute-start(f32[32,128]{1,0:T(8,128)S(1)} %get-tuple-element.43), channel_id=1, source_target_pairs={{0,3},{1,2},{2,1},{3,0},{4,7},{5,6},{6,5},{7,4},{8,11},{9,10},{10,... | collective-permute-start | bytes 49160 | tf_op jit(solution)/shard_map/ppermute | solution.py:43
  9.3 0.9 collective-permute-done.3
  10.2 1.6 collective-permute-done.2
  11.8 3.1 %collective-permute-start.4 = (f32[32,128]{1,0:T(8,128)S(1)}, f32[32,128]{1,0:T(8,128)S(1)}, u32[]{:S(2)}, u32[]{:S(2)}) collective-permute-start(f32[32,128]{1,0:T(8,128)S(1)} %add_add_fusion.a_ref), channel_id=1, source_target_pairs={{0,4},{1,5},{2,6},{3,7},{4,8},{5,9},{6,10},{7,11},{8,12},{9,13},{1... | collective-permute-start | bytes 49160 | tf_op jit(solution)/shard_map/ppermute | solution.py:43
  14.9 4.2 %collective-permute-start.5 = (f32[32,128]{1,0:T(8,128)S(1)}, f32[32,128]{1,0:T(8,128)S(1)}, u32[]{:S(2)}, u32[]{:S(2)}) collective-permute-start(f32[32,128]{1,0:T(8,128)S(1)} %add_add_fusion.a_ref), channel_id=1, source_target_pairs={{0,8},{1,9},{2,10},{3,11},{4,12},{5,13},{6,14},{7,15},{8,0},{9,1},... | collective-permute-start | bytes 49160 | tf_op jit(solution)/shard_map/ppermute | solution.py:43
  19.1 2.4 %collective-permute-start.6 = (f32[32,128]{1,0:T(8,128)S(1)}, f32[32,128]{1,0:T(8,128)S(1)}, u32[]{:S(2)}, u32[]{:S(2)}) collective-permute-start(f32[32,128]{1,0:T(8,128)S(1)} %add_add_fusion.a_ref), channel_id=1, source_target_pairs={{0,12},{1,13},{2,14},{3,15},{4,0},{5,1},{6,2},{7,3},{8,4},{9,5},{1... | collective-permute-start | bytes 49160 | tf_op jit(solution)/shard_map/ppermute | solution.py:43
  21.5 1.3 collective-permute-done.6.d_ref
  22.9 1.2 end_state.1
  24.0 1.7 collective-permute-start.7
  25.7 2.6 %collective-permute-start.8 = (bf16[32,512]{1,0:T(8,128)(2,1)S(1)}, bf16[32,512]{1,0:T(8,128)(2,1)S(1)}, u32[]{:S(2)}, u32[]{:S(2)}) collective-permute-start(bf16[32,512]{1,0:T(8,128)(2,1)S(1)} %get-tuple-element.46.a_ref), channel_id=1, source_target_pairs={{0,32},{16,48},{32,0},{48,16},{64,96},{80,112},{96,64},{112,80},{1... | collective-permute-start | bytes 98312 | tf_op jit(solution)/shard_map/ppermute | solution.py:34
  28.4 1.1 collective-permute-start.9
  29.4 0.6 collective-permute-done.8.c_ref
  30.0 1.1 collective-permute-done.9.d_ref
  31.3 1.6 collective-permute-start.10
  32.9 2.5 %collective-permute-start.11 = (bf16[32,512]{1,0:T(8,128)(2,1)S(1)}, bf16[32,512]{1,0:T(8,128)(2,1)S(1)}, u32[]{:S(2)}, u32[]{:S(2)}) collective-permute-start(bf16[32,512]{1,0:T(8,128)(2,1)S(1)} %get-tuple-element.47.refs_0_), channel_id=1, source_target_pairs={{0,128},{16,144},{32,160},{48,176},{64,192},{80,208},{96,224},{112... | collective-permute-start | bytes 98312 | tf_op jit(solution)/shard_map/ppermute | solution.py:34
  35.3 1.2 collective-permute-start.12
  36.5 0.7 collective-permute-done.11.refs_2_
  37.1 0.9 collective-permute-done.12.refs_3_
  38.1 4.3 %scan.1 = (bf16[64,4096]{1,0:T(8,128)(2,1)S(1)}, bf16[64,4096]{1,0:T(8,128)(2,1)S(1)}) custom-call(bf16[128,512]{1,0:T(8,128)(2,1)S(1)} %join.2.rows_ref, bf16[128,512]{1,0:T(8,128)(2,1)S(1)} %get-tuple-element.48.ends_ref, f32[32,128]{1,0:T(8,128)S(1)} %get-tuple-element.49.maps_ref, f32[128,512]{1,0:T(8,128)S(1)} %get-tuple-element.40.codes_ref, ...), custom_call_target="tpu_custom_call" | custom-call | tf_op jit(solution)/shard_map/scan/pallas_call | solution.py:317
  42.4 5.3 %collective-permute-start.13 = (bf16[64,4096]{1,0:T(8,128)(2,1)S(1)}, bf16[64,4096]{1,0:T(8,128)(2,1)S(1)}, u32[]{:S(2)}, u32[]{:S(2)}) collective-permute-start(bf16[64,4096]{1,0:T(8,128)(2,1)S(1)} %get-tuple-element.54), channel_id=1, source_target_pairs={{0,1},{1,0},{2,3},{3,2},{4,5},{5,4},{6,7},{7,6},{8,9},{9,8},{10,11... | collective-permute-start | bytes 1572872 | tf_op jit(solution)/shard_map/ppermute | solution.py:43
  48.3 1.0 collective-permute-done.13
  49.4 0.8 collective-permute-start.14
  50.2 2.5 %collective-permute-start.15 = (bf16[16,4096]{1,0:T(8,128)(2,1)S(1)}, bf16[16,4096]{1,0:T(8,128)(2,1)S(1)}, u32[]{:S(2)}, u32[]{:S(2)}) collective-permute-start(bf16[16,4096]{1,0:T(8,128)(2,1)S(1)} %get-tuple-element.92), channel_id=1, source_target_pairs={{0,14},{1,15},{2,0},{3,1},{4,2},{5,3},{6,4},{7,5},{8,6},{9,7},{10,... | collective-permute-start | bytes 393224 | tf_op jit(solution)/shard_map/ppermute | solution.py:43
  52.9 2.4 %collective-permute-start.17 = (bf16[8,4096]{1,0:T(8,128)(2,1)S(1)}, bf16[8,4096]{1,0:T(8,128)(2,1)S(1)}, u32[]{:S(2)}, u32[]{:S(2)}) collective-permute-start(bf16[8,4096]{1,0:T(8,128)(2,1)S(1)} %slice.155), channel_id=1, source_target_pairs={{0,8},{1,9},{2,10},{3,11},{4,12},{5,13},{6,14},{7,15},{8,0},{9,1},... | collective-permute-start | bytes 196616 | tf_op jit(solution)/shard_map/ppermute | solution.py:43
  55.3 1.0 collective-permute-done.14
  56.3 2.1 %collective-permute-start.18 = (bf16[8,4096]{1,0:T(8,128)(2,1)S(1)}, bf16[8,4096]{1,0:T(8,128)(2,1)S(1)}, u32[]{:S(2)}, u32[]{:S(2)}) collective-permute-start(bf16[8,4096]{1,0:T(8,128)(2,1)S(1)} %get-tuple-element.90), channel_id=1, source_target_pairs={{0,12},{1,13},{2,14},{3,15},{4,0},{5,1},{6,2},{7,3},{8,4},{9,5},{1... | collective-permute-start | bytes 196616 | tf_op jit(solution)/shard_map/ppermute | solution.py:43
  58.8 1.4 collective-permute-done.17
  60.2 3.9 %collective-permute-done.18 = bf16[8,4096]{1,0:T(8,128)(2,1)S(1)} collective-permute-done((bf16[8,4096]{1,0:T(8,128)(2,1)S(1)}, bf16[8,4096]{1,0:T(8,128)(2,1)S(1)}, u32[]{:S(2)}, u32[]{:S(2)}) %collective-permute-start.18) | collective-permute-done | bytes 65568 | tf_op jit(solution)/shard_map/ppermute | solution.py:43
  64.8 18.5 %all_to_all.10 = bf16[16,2,4096]{2,1,0:T(2,128)(2,1)S(1)} all-to-all(bf16[16,2,4096]{2,1,0:T(2,128)(2,1)S(1)} %reshape.26), channel_id=1, replica_groups=mesh['ctx'=16,'exp'=16] {'exp'}, dimensions={0} | all-to-all | bytes 524288 | tf_op jit(solution)/shard_map/all_to_all | solution.py:546
  84.2 1.5 collective-permute-start.19
  85.7 2.2 %collective-permute-start.20 = (bf16[32,4096]{1,0:T(8,128)(2,1)S(1)}, bf16[32,4096]{1,0:T(8,128)(2,1)S(1)}, u32[]{:S(2)}, u32[]{:S(2)}) collective-permute-start(bf16[32,4096]{1,0:T(8,128)(2,1)S(1)} %pad_maximum_fusion.1), channel_id=1, source_target_pairs={{0,128},{1,33},{2,130},{3,35},{4,132},{5,37},{6,134},{7,39},{8,136... | collective-permute-start | bytes 786440 | tf_op jit(solution)/shard_map/ppermute | solution.py:455
  88.2 2.8 %collective-permute-done.19 = bf16[32,4096]{1,0:T(8,128)(2,1)S(1)} collective-permute-done((bf16[32,4096]{1,0:T(8,128)(2,1)S(1)}, bf16[32,4096]{1,0:T(8,128)(2,1)S(1)}, u32[]{:S(2)}, u32[]{:S(2)}) %collective-permute-start.19) | collective-permute-done | bytes 262176 | tf_op jit(solution)/shard_map/ppermute | solution.py:455
  91.0 3.7 %collective-permute-done.20 = bf16[32,4096]{1,0:T(8,128)(2,1)S(1)} collective-permute-done((bf16[32,4096]{1,0:T(8,128)(2,1)S(1)}, bf16[32,4096]{1,0:T(8,128)(2,1)S(1)}, u32[]{:S(2)}, u32[]{:S(2)}) %collective-permute-start.20) | collective-permute-done | bytes 262176 | tf_op jit(solution)/shard_map/ppermute | solution.py:455
  95.1 2.7 %collective-permute-start.26 = (bf16[64,4096]{1,0:T(8,128)(2,1)S(1)}, bf16[64,4096]{1,0:T(8,128)(2,1)S(1)}, u32[]{:S(2)}, u32[]{:S(2)}) collective-permute-start(bf16[64,4096]{1,0:T(8,128)(2,1)S(1)} %get-tuple-element.79), channel_id=1, source_target_pairs={{0,48},{1,193},{2,50},{3,195},{4,52},{5,197},{6,54},{7,199},{8,56}... | collective-permute-start | bytes 1572872 | tf_op jit(solution)/shard_map/ppermute | solution.py:455
  97.8 1.0 collective-permute-start.24
  98.8 2.3 %collective-permute-start.23 = (bf16[64,4096]{1,0:T(8,128)(2,1)S(1)}, bf16[64,4096]{1,0:T(8,128)(2,1)S(1)}, u32[]{:S(2)}, u32[]{:S(2)}) collective-permute-start(bf16[64,4096]{1,0:T(8,128)(2,1)S(1)} %get-tuple-element.80.refs_0_), channel_id=1, source_target_pairs={{0,48},{1,193},{2,50},{3,195},{4,52},{5,197},{6,54},{7,199},{8,56}... | collective-permute-start | bytes 1572872 | tf_op jit(solution)/shard_map/ppermute | solution.py:455
  101.1 3.5 %fetch.1 = (bf16[4096,512]{1,0:T(8,128)(2,1)S(1)}, bf16[512,4096]{1,0:T(8,128)(2,1)S(1)}) custom-call(bf16[128,4096]{1,0:T(8,128)(2,1)S(1)} %join.3.after_ref, bf16[4096,512]{1,0:T(8,128)(2,1)} %bitcast.16, bf16[512,4096]{1,0:T(8,128)(2,1)} %bitcast.17), custom_call_target="tpu_custom_call" | custom-call | bytes 33554432 | tf_op jit(solution)/shard_map/fetch/pallas_call | solution.py:424
  104.6 1.9 collective-permute-start.27
  106.4 4.0 %expert.3 = (bf16[64,4096]{1,0:T(8,128)(2,1)S(1)}, bf16[64,4096]{1,0:T(8,128)(2,1)S(1)}) custom-call(bf16[64,4096]{1,0:T(8,128)(2,1)S(1)} %get-tuple-element.80.refs_0_, bf16[64,4096]{1,0:T(8,128)(2,1)S(1)} %collective-permute-done.24.refs_1_, bf16[4096,512]{1,0:T(8,128)(2,1)S(1)} %get-tuple-element.62.refs_2_.refs_4_, ...), custom_call_target="tpu_custom_call" | custom-call | flops 1073741824 | bytes 2097152 | tf_op jit(solution)/shard_map/expert/pallas_call | solution.py:400
  110.5 0.6 collective-permute-start.28
  111.1 2.5 %collective-permute-start.29 = (bf16[64,4096]{1,0:T(8,128)(2,1)S(1)}, bf16[64,4096]{1,0:T(8,128)(2,1)S(1)}, u32[]{:S(2)}, u32[]{:S(2)}) collective-permute-start(bf16[64,4096]{1,0:T(8,128)(2,1)S(1)} %collective-permute-done.27.refs_3_), channel_id=1, source_target_pairs={{0,192},{1,49},{2,194},{3,51},{4,196},{5,53},{6,198},{7,55},{8,200... | collective-permute-start | bytes 1572872 | tf_op jit(solution)/shard_map/ppermute | solution.py:455
  113.6 1.6 collective-permute-start.25
  115.2 4.9 %collective-permute-done.28.refs_0_ = bf16[64,4096]{1,0:T(8,128)(2,1)S(1)} collective-permute-done((bf16[64,4096]{1,0:T(8,128)(2,1)S(1)}, bf16[64,4096]{1,0:T(8,128)(2,1)S(1)}, u32[]{:S(2)}, u32[]{:S(2)}) %collective-permute-start.28) | collective-permute-done | bytes 524320 | tf_op jit(solution)/shard_map/ppermute | solution.py:455
  120.1 4.0 %expert.5 = (bf16[64,4096]{1,0:T(8,128)(2,1)S(1)}, bf16[64,4096]{1,0:T(8,128)(2,1)S(1)}) custom-call(bf16[64,4096]{1,0:T(8,128)(2,1)S(1)} %collective-permute-done.28.refs_0_, bf16[64,4096]{1,0:T(8,128)(2,1)S(1)} %collective-permute-done.29.refs_1_, bf16[4096,512]{1,0:T(8,128)(2,1)S(1)} %get-tuple-element.62.refs_2_.refs_4_, ...), custom_call_target="tpu_custom_call" | custom-call | flops 1073741824 | bytes 2097152 | tf_op jit(solution)/shard_map/expert/pallas_call | solution.py:400
  124.1 1.8 collective-permute-start.30
  126.2 5.2 %expert.4 = (bf16[64,4096]{1,0:T(8,128)(2,1)S(1)}, bf16[64,4096]{1,0:T(8,128)(2,1)S(1)}, bf16[64,4096]{1,0:T(8,128)(2,1)S(1)}, bf16[64,4096]{1,0:T(8,128)(2,1)S(1)}) custom-call(bf16[64,4096]{1,0:T(8,128)(2,1)S(1)} %get-tuple-element.78.refs_0_, bf16[64,4096]{1,0:T(8,128)(2,1)S(1)} %collective-permute-done.23.refs_1_, ...), custom_call_target="tpu_custom_call" | custom-call | flops 2147483648 | bytes 4194304 | tf_op jit(solution)/shard_map/expert/pallas_call | solution.py:400
  131.3 3.5 %collective-permute-start.32 = (bf16[64,4096]{1,0:T(8,128)(2,1)S(1)}, bf16[64,4096]{1,0:T(8,128)(2,1)S(1)}, u32[]{:S(2)}, u32[]{:S(2)}) collective-permute-start(bf16[64,4096]{1,0:T(8,128)(2,1)S(1)} %get-tuple-element.68), channel_id=1, source_target_pairs={{0,1},{1,0},{2,3},{3,2},{4,5},{5,4},{6,7},{7,6},{8,9},{9,8},{10,11... | collective-permute-start | bytes 1572872 | tf_op jit(solution)/shard_map/ppermute | solution.py:43
  134.8 1.4 collective-permute-done.31
  136.3 3.5 %collective-permute-start.36 = (bf16[64,4096]{1,0:T(8,128)(2,1)S(1)}, bf16[64,4096]{1,0:T(8,128)(2,1)S(1)}, u32[]{:S(2)}, u32[]{:S(2)}) collective-permute-start(bf16[64,4096]{1,0:T(8,128)(2,1)S(1)} %add_convert_fusion.1), channel_id=1, source_target_pairs={{0,1},{1,0},{2,3},{3,2},{4,5},{5,4},{6,7},{7,6},{8,9},{9,8},{10,11... | collective-permute-start | bytes 1572872 | tf_op jit(solution)/shard_map/ppermute | solution.py:43
  140.0 1.8 collective-permute-start.33
  142.2 1.6 collective-permute-done.35
  143.8 7.6 %collective-permute-done.34 = bf16[64,4096]{1,0:T(8,128)(2,1)S(1)} collective-permute-done((bf16[64,4096]{1,0:T(8,128)(2,1)S(1)}, bf16[64,4096]{1,0:T(8,128)(2,1)S(1)}, u32[]{:S(2)}, u32[]{:S(2)}) %collective-permute-start.34) | collective-permute-done | bytes 524320 | tf_op jit(solution)/shard_map/ppermute | solution.py:455
  151.4 5.6 %collective-permute-done.37 = bf16[64,4096]{1,0:T(8,128)(2,1)S(1)} collective-permute-done((bf16[64,4096]{1,0:T(8,128)(2,1)S(1)}, bf16[64,4096]{1,0:T(8,128)(2,1)S(1)}, u32[]{:S(2)}, u32[]{:S(2)}) %collective-permute-start.37) | collective-permute-done | bytes 524320 | tf_op jit(solution)/shard_map/ppermute | solution.py:455
  157.8 2.2 %collective-permute-start.39 = (bf16[32,4096]{1,0:T(8,128)(2,1)S(1)}, bf16[32,4096]{1,0:T(8,128)(2,1)S(1)}, u32[]{:S(2)}, u32[]{:S(2)}) collective-permute-start(bf16[32,4096]{1,0:T(8,128)(2,1)S(1)} %pad_maximum_fusion.3), channel_id=1, source_target_pairs={{0,128},{1,33},{2,130},{3,35},{4,132},{5,37},{6,134},{7,39},{8,136... | collective-permute-start | bytes 786440 | tf_op jit(solution)/shard_map/ppermute | solution.py:455
  160.0 0.7 collective-permute-start.38
  160.7 6.5 %collective-permute-done.40 = bf16[32,4096]{1,0:T(8,128)(2,1)S(1)} collective-permute-done((bf16[32,4096]{1,0:T(8,128)(2,1)S(1)}, bf16[32,4096]{1,0:T(8,128)(2,1)S(1)}, u32[]{:S(2)}, u32[]{:S(2)}) %collective-permute-start.40) | collective-permute-done | bytes 262176 | tf_op jit(solution)/shard_map/ppermute | solution.py:455
  167.3 0.7 collective-permute-done.38
  168.2 1.0 copy.47
  169.2 5.8 %all-to-all-start.1 = ((bf16[16,2,4096]{2,1,0:T(2,128)(2,1)}), bf16[16,2,4096]{2,1,0:T(2,128)(2,1)S(1)}, u32[]{:S(2)}, u32[]{:S(2)}) async-start(bf16[16,2,4096]{2,1,0:T(2,128)(2,1)} %copy.47), calls=%async_computation.1 | async-start | bytes 524288 | tf_op jit(solution)/shard_map/all_to_all | solution.py:549
  175.1 11.7 %all-to-all-done.1 = bf16[16,2,4096]{2,1,0:T(2,128)(2,1)S(1)} async-done(((bf16[16,2,4096]{2,1,0:T(2,128)(2,1)}), bf16[16,2,4096]{2,1,0:T(2,128)(2,1)S(1)}, u32[]{:S(2)}, u32[]{:S(2)}) %all-to-all-start.1) | async-done | bytes 262176 | tf_op jit(solution)/shard_map/all_to_all | solution.py:549
  186.9 0.9 fusion
  (85 shorter events, 6.3 us)
Async XLA Ops:
  0.0 47.7 %copy-start.2 = (s32[8,2]{0,1:T(2,128)S(1)}, s32[8,2]{0,1:T(2,128)}, u32[]{:S(2)}) copy-start(s32[8,2]{0,1:T(2,128)} %param.26) | copy-start | bytes 196
  0.7 5.4 %collective-permute-start = (bf16[3,512]{1,0:T(4,128)(2,1)S(1)}, bf16[3,512]{1,0:T(4,128)(2,1)S(1)}, u32[]{:S(2)}, u32[]{:S(2)}) collective-permute-start(bf16[3,512]{1,0:T(4,128)(2,1)S(1)} %slice.113), channel_id=1, source_target_pairs={{0,16},{16,32},{32,48},{48,64},{64,80},{80,96},{96,112},{112,128},... | collective-permute-start | bytes 9224 | tf_op jit(solution)/shard_map/ppermute | solution.py:25
  6.3 3.9 %collective-permute-start.3 = (f32[32,128]{1,0:T(8,128)S(1)}, f32[32,128]{1,0:T(8,128)S(1)}, u32[]{:S(2)}, u32[]{:S(2)}) collective-permute-start(f32[32,128]{1,0:T(8,128)S(1)} %get-tuple-element.43), channel_id=1, source_target_pairs={{0,3},{1,2},{2,1},{3,0},{4,7},{5,6},{6,5},{7,4},{8,11},{9,10},{10,... | collective-permute-start | bytes 49160 | tf_op jit(solution)/shard_map/ppermute | solution.py:43
  8.8 3.0 %collective-permute-start.2 = (f32[32,128]{1,0:T(8,128)S(1)}, f32[32,128]{1,0:T(8,128)S(1)}, u32[]{:S(2)}, u32[]{:S(2)}) collective-permute-start(f32[32,128]{1,0:T(8,128)S(1)} %get-tuple-element.43), channel_id=1, source_target_pairs={{0,2},{1,3},{2,0},{3,1},{4,6},{5,7},{6,4},{7,5},{8,10},{9,11},{10,... | collective-permute-start | bytes 49160 | tf_op jit(solution)/shard_map/ppermute | solution.py:43
  8.8 3.0 %collective-permute-start.1 = (f32[32,128]{1,0:T(8,128)S(1)}, f32[32,128]{1,0:T(8,128)S(1)}, u32[]{:S(2)}, u32[]{:S(2)}) collective-permute-start(f32[32,128]{1,0:T(8,128)S(1)} %get-tuple-element.43), channel_id=1, source_target_pairs={{0,1},{1,0},{2,3},{3,2},{4,5},{5,4},{6,7},{7,6},{8,9},{9,8},{10,11... | collective-permute-start | bytes 49160 | tf_op jit(solution)/shard_map/ppermute | solution.py:43
  11.8 9.7 %collective-permute-start.4 = (f32[32,128]{1,0:T(8,128)S(1)}, f32[32,128]{1,0:T(8,128)S(1)}, u32[]{:S(2)}, u32[]{:S(2)}) collective-permute-start(f32[32,128]{1,0:T(8,128)S(1)} %add_add_fusion.a_ref), channel_id=1, source_target_pairs={{0,4},{1,5},{2,6},{3,7},{4,8},{5,9},{6,10},{7,11},{8,12},{9,13},{1... | collective-permute-start | bytes 49160 | tf_op jit(solution)/shard_map/ppermute | solution.py:43
  14.9 6.6 %collective-permute-start.5 = (f32[32,128]{1,0:T(8,128)S(1)}, f32[32,128]{1,0:T(8,128)S(1)}, u32[]{:S(2)}, u32[]{:S(2)}) collective-permute-start(f32[32,128]{1,0:T(8,128)S(1)} %add_add_fusion.a_ref), channel_id=1, source_target_pairs={{0,8},{1,9},{2,10},{3,11},{4,12},{5,13},{6,14},{7,15},{8,0},{9,1},... | collective-permute-start | bytes 49160 | tf_op jit(solution)/shard_map/ppermute | solution.py:43
  19.1 3.7 %collective-permute-start.6 = (f32[32,128]{1,0:T(8,128)S(1)}, f32[32,128]{1,0:T(8,128)S(1)}, u32[]{:S(2)}, u32[]{:S(2)}) collective-permute-start(f32[32,128]{1,0:T(8,128)S(1)} %add_add_fusion.a_ref), channel_id=1, source_target_pairs={{0,12},{1,13},{2,14},{3,15},{4,0},{5,1},{6,2},{7,3},{8,4},{9,5},{1... | collective-permute-start | bytes 49160 | tf_op jit(solution)/shard_map/ppermute | solution.py:43
  24.0 5.4 %collective-permute-start.7 = (bf16[32,512]{1,0:T(8,128)(2,1)S(1)}, bf16[32,512]{1,0:T(8,128)(2,1)S(1)}, u32[]{:S(2)}, u32[]{:S(2)}) collective-permute-start(bf16[32,512]{1,0:T(8,128)(2,1)S(1)} %get-tuple-element.46.a_ref), channel_id=1, source_target_pairs={{0,16},{16,32},{32,48},{48,0},{64,80},{80,96},{96,112},{112,64},{1... | collective-permute-start | bytes 98312 | tf_op jit(solution)/shard_map/ppermute | solution.py:34
  25.7 4.3 %collective-permute-start.8 = (bf16[32,512]{1,0:T(8,128)(2,1)S(1)}, bf16[32,512]{1,0:T(8,128)(2,1)S(1)}, u32[]{:S(2)}, u32[]{:S(2)}) collective-permute-start(bf16[32,512]{1,0:T(8,128)(2,1)S(1)} %get-tuple-element.46.a_ref), channel_id=1, source_target_pairs={{0,32},{16,48},{32,0},{48,16},{64,96},{80,112},{96,64},{112,80},{1... | collective-permute-start | bytes 98312 | tf_op jit(solution)/shard_map/ppermute | solution.py:34
  28.4 2.8 %collective-permute-start.9 = (bf16[32,512]{1,0:T(8,128)(2,1)S(1)}, bf16[32,512]{1,0:T(8,128)(2,1)S(1)}, u32[]{:S(2)}, u32[]{:S(2)}) collective-permute-start(bf16[32,512]{1,0:T(8,128)(2,1)S(1)} %get-tuple-element.46.a_ref), channel_id=1, source_target_pairs={{0,48},{16,0},{32,16},{48,32},{64,112},{80,64},{96,80},{112,96},{1... | collective-permute-start | bytes 98312 | tf_op jit(solution)/shard_map/ppermute | solution.py:34
  31.3 5.2 %collective-permute-start.10 = (bf16[32,512]{1,0:T(8,128)(2,1)S(1)}, bf16[32,512]{1,0:T(8,128)(2,1)S(1)}, u32[]{:S(2)}, u32[]{:S(2)}) collective-permute-start(bf16[32,512]{1,0:T(8,128)(2,1)S(1)} %get-tuple-element.47.refs_0_), channel_id=1, source_target_pairs={{0,64},{16,80},{32,96},{48,112},{64,128},{80,144},{96,160},{112,17... | collective-permute-start | bytes 98312 | tf_op jit(solution)/shard_map/ppermute | solution.py:34
  32.9 4.3 %collective-permute-start.11 = (bf16[32,512]{1,0:T(8,128)(2,1)S(1)}, bf16[32,512]{1,0:T(8,128)(2,1)S(1)}, u32[]{:S(2)}, u32[]{:S(2)}) collective-permute-start(bf16[32,512]{1,0:T(8,128)(2,1)S(1)} %get-tuple-element.47.refs_0_), channel_id=1, source_target_pairs={{0,128},{16,144},{32,160},{48,176},{64,192},{80,208},{96,224},{112... | collective-permute-start | bytes 98312 | tf_op jit(solution)/shard_map/ppermute | solution.py:34
  35.3 2.8 %collective-permute-start.12 = (bf16[32,512]{1,0:T(8,128)(2,1)S(1)}, bf16[32,512]{1,0:T(8,128)(2,1)S(1)}, u32[]{:S(2)}, u32[]{:S(2)}) collective-permute-start(bf16[32,512]{1,0:T(8,128)(2,1)S(1)} %get-tuple-element.47.refs_0_), channel_id=1, source_target_pairs={{0,192},{16,208},{32,224},{48,240},{64,0},{80,16},{96,32},{112,48}... | collective-permute-start | bytes 98312 | tf_op jit(solution)/shard_map/ppermute | solution.py:34
  38.1 26.0 %copy-start = (bf16[8,4096]{1,0:T(8,128)(2,1)S(1)}, bf16[8,4096]{1,0:T(8,128)(2,1)}, u32[]{:S(2)}) copy-start(bf16[8,4096]{1,0:T(8,128)(2,1)} %param.24) | copy-start | bytes 196612
  38.1 26.2 %copy-start.1 = (f32[4096]{0:T(1024)S(1)}, f32[4096]{0:T(1024)}, u32[]{:S(2)}) copy-start(f32[4096]{0:T(1024)} %param.25) | copy-start | bytes 49156
  42.4 6.9 %collective-permute-start.13 = (bf16[64,4096]{1,0:T(8,128)(2,1)S(1)}, bf16[64,4096]{1,0:T(8,128)(2,1)S(1)}, u32[]{:S(2)}, u32[]{:S(2)}) collective-permute-start(bf16[64,4096]{1,0:T(8,128)(2,1)S(1)} %get-tuple-element.54), channel_id=1, source_target_pairs={{0,1},{1,0},{2,3},{3,2},{4,5},{5,4},{6,7},{7,6},{8,9},{9,8},{10,11... | collective-permute-start | bytes 1572872 | tf_op jit(solution)/shard_map/ppermute | solution.py:43
  49.4 6.8 %collective-permute-start.14 = (bf16[16,4096]{1,0:T(8,128)(2,1)S(1)}, bf16[16,4096]{1,0:T(8,128)(2,1)S(1)}, u32[]{:S(2)}, u32[]{:S(2)}) collective-permute-start(bf16[16,4096]{1,0:T(8,128)(2,1)S(1)} %get-tuple-element.91), channel_id=1, source_target_pairs={{0,2},{1,3},{2,4},{3,5},{4,6},{5,7},{6,8},{7,9},{8,10},{9,11},{10,... | collective-permute-start | bytes 393224 | tf_op jit(solution)/shard_map/ppermute | solution.py:43
  50.2 6.0 %collective-permute-start.15 = (bf16[16,4096]{1,0:T(8,128)(2,1)S(1)}, bf16[16,4096]{1,0:T(8,128)(2,1)S(1)}, u32[]{:S(2)}, u32[]{:S(2)}) collective-permute-start(bf16[16,4096]{1,0:T(8,128)(2,1)S(1)} %get-tuple-element.92), channel_id=1, source_target_pairs={{0,14},{1,15},{2,0},{3,1},{4,2},{5,3},{6,4},{7,5},{8,6},{9,7},{10,... | collective-permute-start | bytes 393224 | tf_op jit(solution)/shard_map/ppermute | solution.py:43
  52.9 7.3 %collective-permute-start.17 = (bf16[8,4096]{1,0:T(8,128)(2,1)S(1)}, bf16[8,4096]{1,0:T(8,128)(2,1)S(1)}, u32[]{:S(2)}, u32[]{:S(2)}) collective-permute-start(bf16[8,4096]{1,0:T(8,128)(2,1)S(1)} %slice.155), channel_id=1, source_target_pairs={{0,8},{1,9},{2,10},{3,11},{4,12},{5,13},{6,14},{7,15},{8,0},{9,1},... | collective-permute-start | bytes 196616 | tf_op jit(solution)/shard_map/ppermute | solution.py:43
  56.3 7.8 %collective-permute-start.18 = (bf16[8,4096]{1,0:T(8,128)(2,1)S(1)}, bf16[8,4096]{1,0:T(8,128)(2,1)S(1)}, u32[]{:S(2)}, u32[]{:S(2)}) collective-permute-start(bf16[8,4096]{1,0:T(8,128)(2,1)S(1)} %get-tuple-element.90), channel_id=1, source_target_pairs={{0,12},{1,13},{2,14},{3,15},{4,0},{5,1},{6,2},{7,3},{8,4},{9,5},{1... | collective-permute-start | bytes 196616 | tf_op jit(solution)/shard_map/ppermute | solution.py:43
  58.3 5.7 %collective-permute-start.16 = (bf16[8,4096]{1,0:T(8,128)(2,1)S(1)}, bf16[8,4096]{1,0:T(8,128)(2,1)S(1)}, u32[]{:S(2)}, u32[]{:S(2)}) collective-permute-start(bf16[8,4096]{1,0:T(8,128)(2,1)S(1)} %get-tuple-element.89), channel_id=1, source_target_pairs={{0,4},{1,5},{2,6},{3,7},{4,8},{5,9},{6,10},{7,11},{8,12},{9,13},{1... | collective-permute-start | bytes 196616 | tf_op jit(solution)/shard_map/ppermute | solution.py:43
  84.2 6.8 %collective-permute-start.19 = (bf16[32,4096]{1,0:T(8,128)(2,1)S(1)}, bf16[32,4096]{1,0:T(8,128)(2,1)S(1)}, u32[]{:S(2)}, u32[]{:S(2)}) collective-permute-start(bf16[32,4096]{1,0:T(8,128)(2,1)S(1)} %pad_maximum_fusion.1), channel_id=1, source_target_pairs={{0,64},{1,17},{2,66},{3,19},{4,68},{5,21},{6,70},{7,23},{8,72},{9,... | collective-permute-start | bytes 786440 | tf_op jit(solution)/shard_map/ppermute | solution.py:455
  85.7 9.1 %collective-permute-start.20 = (bf16[32,4096]{1,0:T(8,128)(2,1)S(1)}, bf16[32,4096]{1,0:T(8,128)(2,1)S(1)}, u32[]{:S(2)}, u32[]{:S(2)}) collective-permute-start(bf16[32,4096]{1,0:T(8,128)(2,1)S(1)} %pad_maximum_fusion.1), channel_id=1, source_target_pairs={{0,128},{1,33},{2,130},{3,35},{4,132},{5,37},{6,134},{7,39},{8,136... | collective-permute-start | bytes 786440 | tf_op jit(solution)/shard_map/ppermute | solution.py:455
  87.9 6.9 %collective-permute-start.21 = (bf16[32,4096]{1,0:T(8,128)(2,1)S(1)}, bf16[32,4096]{1,0:T(8,128)(2,1)S(1)}, u32[]{:S(2)}, u32[]{:S(2)}) collective-permute-start(bf16[32,4096]{1,0:T(8,128)(2,1)S(1)} %pad_maximum_fusion.1), channel_id=1, source_target_pairs={{0,192},{1,49},{2,194},{3,51},{4,196},{5,53},{6,198},{7,55},{8,200... | collective-permute-start | bytes 786440 | tf_op jit(solution)/shard_map/ppermute | solution.py:455
  94.9 15.5 %collective-permute-start.22 = (bf16[128,4096]{1,0:T(8,128)(2,1)S(1)}, bf16[128,4096]{1,0:T(8,128)(2,1)S(1)}, u32[]{:S(2)}, u32[]{:S(2)}) collective-permute-start(bf16[128,4096]{1,0:T(8,128)(2,1)S(1)} %join.3.after_ref), channel_id=1, source_target_pairs={{0,16},{1,65},{2,18},{3,67},{4,20},{5,69},{6,22},{7,71},{8,24},{9,... | collective-permute-start | bytes 3145736 | tf_op jit(solution)/shard_map/ppermute | solution.py:455
  95.1 9.5 %collective-permute-start.26 = (bf16[64,4096]{1,0:T(8,128)(2,1)S(1)}, bf16[64,4096]{1,0:T(8,128)(2,1)S(1)}, u32[]{:S(2)}, u32[]{:S(2)}) collective-permute-start(bf16[64,4096]{1,0:T(8,128)(2,1)S(1)} %get-tuple-element.79), channel_id=1, source_target_pairs={{0,48},{1,193},{2,50},{3,195},{4,52},{5,197},{6,54},{7,199},{8,56}... | collective-permute-start | bytes 1572872 | tf_op jit(solution)/shard_map/ppermute | solution.py:455
  97.8 8.6 %collective-permute-start.24 = (bf16[64,4096]{1,0:T(8,128)(2,1)S(1)}, bf16[64,4096]{1,0:T(8,128)(2,1)S(1)}, u32[]{:S(2)}, u32[]{:S(2)}) collective-permute-start(bf16[64,4096]{1,0:T(8,128)(2,1)S(1)} %get-tuple-element.79), channel_id=1, source_target_pairs={{0,1},{1,0},{2,3},{3,2},{4,5},{5,4},{6,7},{7,6},{8,9},{9,8},{10,11... | collective-permute-start | bytes 1572872 | tf_op jit(solution)/shard_map/ppermute | solution.py:43
  98.8 11.6 %collective-permute-start.23 = (bf16[64,4096]{1,0:T(8,128)(2,1)S(1)}, bf16[64,4096]{1,0:T(8,128)(2,1)S(1)}, u32[]{:S(2)}, u32[]{:S(2)}) collective-permute-start(bf16[64,4096]{1,0:T(8,128)(2,1)S(1)} %get-tuple-element.80.refs_0_), channel_id=1, source_target_pairs={{0,48},{1,193},{2,50},{3,195},{4,52},{5,197},{6,54},{7,199},{8,56}... | collective-permute-start | bytes 1572872 | tf_op jit(solution)/shard_map/ppermute | solution.py:455
  104.6 6.6 %collective-permute-start.27 = (bf16[64,4096]{1,0:T(8,128)(2,1)S(1)}, bf16[64,4096]{1,0:T(8,128)(2,1)S(1)}, u32[]{:S(2)}, u32[]{:S(2)}) collective-permute-start(bf16[64,4096]{1,0:T(8,128)(2,1)S(1)} %collective-permute-done.26), channel_id=1, source_target_pairs={{0,1},{1,0},{2,3},{3,2},{4,5},{5,4},{6,7},{7,6},{8,9},{9,8},{10,11... | collective-permute-start | bytes 1572872 | tf_op jit(solution)/shard_map/ppermute | solution.py:43
  110.5 9.6 %collective-permute-start.28 = (bf16[64,4096]{1,0:T(8,128)(2,1)S(1)}, bf16[64,4096]{1,0:T(8,128)(2,1)S(1)}, u32[]{:S(2)}, u32[]{:S(2)}) collective-permute-start(bf16[64,4096]{1,0:T(8,128)(2,1)S(1)} %get-tuple-element.78.refs_0_), channel_id=1, source_target_pairs={{0,16},{1,65},{2,18},{3,67},{4,20},{5,69},{6,22},{7,71},{8,24},{9,... | collective-permute-start | bytes 1572872 | tf_op jit(solution)/shard_map/ppermute | solution.py:455
  111.1 9.0 %collective-permute-start.29 = (bf16[64,4096]{1,0:T(8,128)(2,1)S(1)}, bf16[64,4096]{1,0:T(8,128)(2,1)S(1)}, u32[]{:S(2)}, u32[]{:S(2)}) collective-permute-start(bf16[64,4096]{1,0:T(8,128)(2,1)S(1)} %collective-permute-done.27.refs_3_), channel_id=1, source_target_pairs={{0,192},{1,49},{2,194},{3,51},{4,196},{5,53},{6,198},{7,55},{8,200... | collective-permute-start | bytes 1572872 | tf_op jit(solution)/shard_map/ppermute | solution.py:455
  113.6 12.5 %collective-permute-start.25 = (bf16[64,4096]{1,0:T(8,128)(2,1)S(1)}, bf16[64,4096]{1,0:T(8,128)(2,1)S(1)}, u32[]{:S(2)}, u32[]{:S(2)}) collective-permute-start(bf16[64,4096]{1,0:T(8,128)(2,1)S(1)} %get-tuple-element.77), channel_id=1, source_target_pairs={{0,1},{1,0},{2,3},{3,2},{4,5},{5,4},{6,7},{7,6},{8,9},{9,8},{10,11... | collective-permute-start | bytes 1572872 | tf_op jit(solution)/shard_map/ppermute | solution.py:43
  124.1 10.7 %collective-permute-start.30 = (bf16[64,4096]{1,0:T(8,128)(2,1)S(1)}, bf16[64,4096]{1,0:T(8,128)(2,1)S(1)}, u32[]{:S(2)}, u32[]{:S(2)}) collective-permute-start(bf16[64,4096]{1,0:T(8,128)(2,1)S(1)} %get-tuple-element.65), channel_id=1, source_target_pairs={{0,48},{1,193},{2,50},{3,195},{4,52},{5,197},{6,54},{7,199},{8,56}... | collective-permute-start | bytes 1572872 | tf_op jit(solution)/shard_map/ppermute | solution.py:455
  125.9 10.3 %collective-permute-start.31 = (bf16[64,4096]{1,0:T(8,128)(2,1)S(1)}, bf16[64,4096]{1,0:T(8,128)(2,1)S(1)}, u32[]{:S(2)}, u32[]{:S(2)}) collective-permute-start(bf16[64,4096]{1,0:T(8,128)(2,1)S(1)} %get-tuple-element.66), channel_id=1, source_target_pairs={{0,64},{1,17},{2,66},{3,19},{4,68},{5,21},{6,70},{7,23},{8,72},{9,... | collective-permute-start | bytes 1572872 | tf_op jit(solution)/shard_map/ppermute | solution.py:455
  131.3 8.6 %collective-permute-start.32 = (bf16[64,4096]{1,0:T(8,128)(2,1)S(1)}, bf16[64,4096]{1,0:T(8,128)(2,1)S(1)}, u32[]{:S(2)}, u32[]{:S(2)}) collective-permute-start(bf16[64,4096]{1,0:T(8,128)(2,1)S(1)} %get-tuple-element.68), channel_id=1, source_target_pairs={{0,1},{1,0},{2,3},{3,2},{4,5},{5,4},{6,7},{7,6},{8,9},{9,8},{10,11... | collective-permute-start | bytes 1572872 | tf_op jit(solution)/shard_map/ppermute | solution.py:43
  136.3 5.6 %collective-permute-start.36 = (bf16[64,4096]{1,0:T(8,128)(2,1)S(1)}, bf16[64,4096]{1,0:T(8,128)(2,1)S(1)}, u32[]{:S(2)}, u32[]{:S(2)}) collective-permute-start(bf16[64,4096]{1,0:T(8,128)(2,1)S(1)} %add_convert_fusion.1), channel_id=1, source_target_pairs={{0,1},{1,0},{2,3},{3,2},{4,5},{5,4},{6,7},{7,6},{8,9},{9,8},{10,11... | collective-permute-start | bytes 1572872 | tf_op jit(solution)/shard_map/ppermute | solution.py:43
  140.0 17.0 %collective-permute-start.33 = (bf16[128,4096]{1,0:T(8,128)(2,1)S(1)}, bf16[128,4096]{1,0:T(8,128)(2,1)S(1)}, u32[]{:S(2)}, u32[]{:S(2)}) collective-permute-start(bf16[128,4096]{1,0:T(8,128)(2,1)S(1)} %pad_maximum_fusion), channel_id=1, source_target_pairs={{0,48},{1,193},{2,50},{3,195},{4,52},{5,197},{6,54},{7,199},{8,56}... | collective-permute-start | bytes 3145736 | tf_op jit(solution)/shard_map/ppermute | solution.py:455
  141.9 1.9 %collective-permute-start.35 = (bf16[64,4096]{1,0:T(8,128)(2,1)S(1)}, bf16[64,4096]{1,0:T(8,128)(2,1)S(1)}, u32[]{:S(2)}, u32[]{:S(2)}) collective-permute-start(bf16[64,4096]{1,0:T(8,128)(2,1)S(1)} %get-tuple-element.70), channel_id=1, source_target_pairs={{0,1},{1,0},{2,3},{3,2},{4,5},{5,4},{6,7},{7,6},{8,9},{9,8},{10,11... | collective-permute-start | bytes 1572872 | tf_op jit(solution)/shard_map/ppermute | solution.py:43
  141.9 9.5 %collective-permute-start.34 = (bf16[64,4096]{1,0:T(8,128)(2,1)S(1)}, bf16[64,4096]{1,0:T(8,128)(2,1)S(1)}, u32[]{:S(2)}, u32[]{:S(2)}) collective-permute-start(bf16[64,4096]{1,0:T(8,128)(2,1)S(1)} %get-tuple-element.69), channel_id=1, source_target_pairs={{0,16},{1,65},{2,18},{3,67},{4,20},{5,69},{6,22},{7,71},{8,24},{9,... | collective-permute-start | bytes 1572872 | tf_op jit(solution)/shard_map/ppermute | solution.py:455
  141.9 15.1 %collective-permute-start.37 = (bf16[64,4096]{1,0:T(8,128)(2,1)S(1)}, bf16[64,4096]{1,0:T(8,128)(2,1)S(1)}, u32[]{:S(2)}, u32[]{:S(2)}) collective-permute-start(bf16[64,4096]{1,0:T(8,128)(2,1)S(1)} %collective-permute-done.36), channel_id=1, source_target_pairs={{0,16},{1,65},{2,18},{3,67},{4,20},{5,69},{6,22},{7,71},{8,24},{9,... | collective-permute-start | bytes 1572872 | tf_op jit(solution)/shard_map/ppermute | solution.py:455
  157.5 17.5 %copy-start.3 = (s32[8,2]{0,1:T(2,128)S(1)}, s32[8,2]{0,1:T(2,128)}, u32[]{:S(2)}) copy-start(s32[8,2]{0,1:T(2,128)} %param.27) | copy-start | bytes 196
  157.6 9.6 %collective-permute-start.40 = (bf16[32,4096]{1,0:T(8,128)(2,1)S(1)}, bf16[32,4096]{1,0:T(8,128)(2,1)S(1)}, u32[]{:S(2)}, u32[]{:S(2)}) collective-permute-start(bf16[32,4096]{1,0:T(8,128)(2,1)S(1)} %pad_maximum_fusion.4), channel_id=1, source_target_pairs={{0,64},{1,17},{2,66},{3,19},{4,68},{5,21},{6,70},{7,23},{8,72},{9,... | collective-permute-start | bytes 786440 | tf_op jit(solution)/shard_map/ppermute | solution.py:455
  157.8 9.5 %collective-permute-start.39 = (bf16[32,4096]{1,0:T(8,128)(2,1)S(1)}, bf16[32,4096]{1,0:T(8,128)(2,1)S(1)}, u32[]{:S(2)}, u32[]{:S(2)}) collective-permute-start(bf16[32,4096]{1,0:T(8,128)(2,1)S(1)} %pad_maximum_fusion.3), channel_id=1, source_target_pairs={{0,128},{1,33},{2,130},{3,35},{4,132},{5,37},{6,134},{7,39},{8,136... | collective-permute-start | bytes 786440 | tf_op jit(solution)/shard_map/ppermute | solution.py:455
  160.0 8.0 %collective-permute-start.38 = (bf16[32,4096]{1,0:T(8,128)(2,1)S(1)}, bf16[32,4096]{1,0:T(8,128)(2,1)S(1)}, u32[]{:S(2)}, u32[]{:S(2)}) collective-permute-start(bf16[32,4096]{1,0:T(8,128)(2,1)S(1)} %pad_maximum_fusion.2), channel_id=1, source_target_pairs={{0,192},{1,49},{2,194},{3,51},{4,196},{5,53},{6,198},{7,55},{8,200... | collective-permute-start | bytes 786440 | tf_op jit(solution)/shard_map/ppermute | solution.py:455
  169.2 17.6 %all-to-all-start.1 = ((bf16[16,2,4096]{2,1,0:T(2,128)(2,1)}), bf16[16,2,4096]{2,1,0:T(2,128)(2,1)S(1)}, u32[]{:S(2)}, u32[]{:S(2)}) async-start(bf16[16,2,4096]{2,1,0:T(2,128)(2,1)} %copy.47), calls=%async_computation.1 | async-start | bytes 524288 | tf_op jit(solution)/shard_map/all_to_all | solution.py:549

commit v2 on v1

--- a/solution.py
+++ b/solution.py
@@ -474,9 +474,11 @@
     close = [after[:half], before_mine, swap(after[half:]), before_swapped]
     far_mine, far_swapped = expert([far_mine, far_swapped], up, down)
     passed_mine, passed_swapped = along_side(far_mine, 1, -1), along_side(far_swapped, 0, 1)
-    passed_mine, passed_swapped = lax.optimization_barrier((passed_mine, passed_swapped))
+    passed_mine, passed_swapped, own_theirs = lax.optimization_barrier(
+        (passed_mine, passed_swapped, swap(own_swapped))
+    )
     after_mine, before_mine, after_swapped, before_swapped = expert(close, up, down)
-    own_theirs, after_theirs = swap(own_swapped), swap(after_swapped)
+    after_theirs = swap(after_swapped)
     before_theirs = swap(added(before_swapped, passed_swapped))
     one = along_side(jnp.concatenate([added(after_mine, passed_mine), after_theirs]), 1, -1)
     three_mine, three_theirs = along_side(before_mine, 1, 1), along_side(before_theirs, 1, 1)

time: 188 us -> 187 us (level)
    ppermute x16, waiting for transfers between devices: 33.4 us -> 35.3 us  [along_side(): return lax.ppermute(array, ('ctx', 'exp'), pairs)]
  transfers between devices with their start and end apart: 42 -> 42, of which waited for: 21 -> 20; matrix products, arithmetic and copies ran while one was open for 1% -> 1% of each run, Pallas kernels for 10% -> 10%
where the time goes in v2:
time: 187 us
  starting transfers between devices  76.4 us (41%)
  waiting for transfers between devices  61.5 us (33%)
  Pallas kernels  23.7 us (13%)
  blocking collectives  18.5 us (10%)
  local copies, waits for them, and re-layouts  3.53 us (2%)
  other arithmetic  1.87 us (1%)
    ppermute x18, starting transfers between devices, along_depth(): return lax.ppermute(array, 'exp', pairs)  37.6 us
    ppermute x16, waiting for transfers between devices, along_side(): return lax.ppermute(array, ('ctx', 'exp'), pairs)  35.3 us
    ppermute x16, starting transfers between devices, along_side(): return lax.ppermute(array, ('ctx', 'exp'), pairs)  19.1 us
    all_to_all x1, blocking collectives, shards(): lax.all_to_all(outgoing, 'exp', split_axis=0, concat_axis=0, tiled=True)  18.5 us
    pallas_call x3, Pallas kernels, expert(): pl.pallas_call(functools.partial(expert_kernel, len(pieces)), out_shape=t...  13.1 us
    all_to_all x1, waiting for transfers between devices, shards(): lax.all_to_all(expert_out, 'exp', split_axis=0, concat_axis=0, tiled=True)  11.7 us
    ppermute x18, waiting for transfers between devices, along_depth(): return lax.ppermute(array, 'exp', pairs)  11.2 us
    ppermute x6, starting transfers between devices, along_plane(): return lax.ppermute(array, 'ctx', pairs)  10.6 us
  transfers between devices with their start and end apart: 42, of which 20 were waited for; matrix products, arithmetic and copies ran while one was open for 1% of the time, Pallas kernels for 10%

profile of v2, /device:TPU:1, one launch (start us, length us, event | category | flops | bytes accessed | tf_op | source)
XLA Modules:
  0.0 187.1 jit_solution(1704948051215022798)
XLA Ops:
  0.0 0.7 slice.113
  0.7 4.0 %collective-permute-start = (bf16[3,512]{1,0:T(4,128)(2,1)S(1)}, bf16[3,512]{1,0:T(4,128)(2,1)S(1)}, u32[]{:S(2)}, u32[]{:S(2)}) collective-permute-start(bf16[3,512]{1,0:T(4,128)(2,1)S(1)} %slice.113), channel_id=1, source_target_pairs={{0,16},{16,32},{32,48},{48,64},{64,80},{80,96},{96,112},{112,128},... | collective-permute-start | bytes 9224 | tf_op jit(solution)/shard_map/ppermute | solution.py:25
  4.7 1.3 stage.1
  6.3 2.5 %collective-permute-start.3 = (f32[32,128]{1,0:T(8,128)S(1)}, f32[32,128]{1,0:T(8,128)S(1)}, u32[]{:S(2)}, u32[]{:S(2)}) collective-permute-start(f32[32,128]{1,0:T(8,128)S(1)} %get-tuple-element.44), channel_id=1, source_target_pairs={{0,3},{1,2},{2,1},{3,0},{4,7},{5,6},{6,5},{7,4},{8,11},{9,10},{10,... | collective-permute-start | bytes 49160 | tf_op jit(solution)/shard_map/ppermute | solution.py:43
  9.3 0.9 collective-permute-done.3
  10.2 1.6 collective-permute-done.2
  11.8 3.1 %collective-permute-start.4 = (f32[32,128]{1,0:T(8,128)S(1)}, f32[32,128]{1,0:T(8,128)S(1)}, u32[]{:S(2)}, u32[]{:S(2)}) collective-permute-start(f32[32,128]{1,0:T(8,128)S(1)} %add_add_fusion.a_ref), channel_id=1, source_target_pairs={{0,4},{1,5},{2,6},{3,7},{4,8},{5,9},{6,10},{7,11},{8,12},{9,13},{1... | collective-permute-start | bytes 49160 | tf_op jit(solution)/shard_map/ppermute | solution.py:43
  14.9 4.2 %collective-permute-start.5 = (f32[32,128]{1,0:T(8,128)S(1)}, f32[32,128]{1,0:T(8,128)S(1)}, u32[]{:S(2)}, u32[]{:S(2)}) collective-permute-start(f32[32,128]{1,0:T(8,128)S(1)} %add_add_fusion.a_ref), channel_id=1, source_target_pairs={{0,8},{1,9},{2,10},{3,11},{4,12},{5,13},{6,14},{7,15},{8,0},{9,1},... | collective-permute-start | bytes 49160 | tf_op jit(solution)/shard_map/ppermute | solution.py:43
  19.1 2.4 %collective-permute-start.6 = (f32[32,128]{1,0:T(8,128)S(1)}, f32[32,128]{1,0:T(8,128)S(1)}, u32[]{:S(2)}, u32[]{:S(2)}) collective-permute-start(f32[32,128]{1,0:T(8,128)S(1)} %add_add_fusion.a_ref), channel_id=1, source_target_pairs={{0,12},{1,13},{2,14},{3,15},{4,0},{5,1},{6,2},{7,3},{8,4},{9,5},{1... | collective-permute-start | bytes 49160 | tf_op jit(solution)/shard_map/ppermute | solution.py:43
  21.5 1.3 collective-permute-done.6.d_ref
  22.9 1.2 end_state.1
  24.0 1.7 collective-permute-start.7
  25.7 2.6 %collective-permute-start.8 = (bf16[32,512]{1,0:T(8,128)(2,1)S(1)}, bf16[32,512]{1,0:T(8,128)(2,1)S(1)}, u32[]{:S(2)}, u32[]{:S(2)}) collective-permute-start(bf16[32,512]{1,0:T(8,128)(2,1)S(1)} %get-tuple-element.47.a_ref), channel_id=1, source_target_pairs={{0,32},{16,48},{32,0},{48,16},{64,96},{80,112},{96,64},{112,80},{1... | collective-permute-start | bytes 98312 | tf_op jit(solution)/shard_map/ppermute | solution.py:34
  28.4 1.1 collective-permute-start.9
  29.4 0.6 collective-permute-done.8.c_ref
  30.0 1.1 collective-permute-done.9.d_ref
  31.3 1.6 collective-permute-start.10
  32.9 2.5 %collective-permute-start.11 = (bf16[32,512]{1,0:T(8,128)(2,1)S(1)}, bf16[32,512]{1,0:T(8,128)(2,1)S(1)}, u32[]{:S(2)}, u32[]{:S(2)}) collective-permute-start(bf16[32,512]{1,0:T(8,128)(2,1)S(1)} %get-tuple-element.48.refs_0_), channel_id=1, source_target_pairs={{0,128},{16,144},{32,160},{48,176},{64,192},{80,208},{96,224},{112... | collective-permute-start | bytes 98312 | tf_op jit(solution)/shard_map/ppermute | solution.py:34
  35.3 1.2 collective-permute-start.12
  36.5 0.7 collective-permute-done.11.refs_2_
  37.1 0.9 collective-permute-done.12.refs_3_
  38.1 4.3 %scan.1 = (bf16[64,4096]{1,0:T(8,128)(2,1)S(1)}, bf16[64,4096]{1,0:T(8,128)(2,1)S(1)}) custom-call(bf16[128,512]{1,0:T(8,128)(2,1)S(1)} %join.2.rows_ref, bf16[128,512]{1,0:T(8,128)(2,1)S(1)} %get-tuple-element.49.ends_ref, f32[32,128]{1,0:T(8,128)S(1)} %get-tuple-element.50.maps_ref, f32[128,512]{1,0:T(8,128)S(1)} %get-tuple-element.41.codes_ref, ...), custom_call_target="tpu_custom_call" | custom-call | tf_op jit(solution)/shard_map/scan/pallas_call | solution.py:317
  42.4 5.3 %collective-permute-start.13 = (bf16[64,4096]{1,0:T(8,128)(2,1)S(1)}, bf16[64,4096]{1,0:T(8,128)(2,1)S(1)}, u32[]{:S(2)}, u32[]{:S(2)}) collective-permute-start(bf16[64,4096]{1,0:T(8,128)(2,1)S(1)} %get-tuple-element.55), channel_id=1, source_target_pairs={{0,1},{1,0},{2,3},{3,2},{4,5},{5,4},{6,7},{7,6},{8,9},{9,8},{10,11... | collective-permute-start | bytes 1572872 | tf_op jit(solution)/shard_map/ppermute | solution.py:43
  48.3 1.0 collective-permute-done.13
  49.4 0.8 collective-permute-start.14
  50.2 2.5 %collective-permute-start.15 = (bf16[16,4096]{1,0:T(8,128)(2,1)S(1)}, bf16[16,4096]{1,0:T(8,128)(2,1)S(1)}, u32[]{:S(2)}, u32[]{:S(2)}) collective-permute-start(bf16[16,4096]{1,0:T(8,128)(2,1)S(1)} %get-tuple-element.94), channel_id=1, source_target_pairs={{0,14},{1,15},{2,0},{3,1},{4,2},{5,3},{6,4},{7,5},{8,6},{9,7},{10,... | collective-permute-start | bytes 393224 | tf_op jit(solution)/shard_map/ppermute | solution.py:43
  52.9 2.4 %collective-permute-start.17 = (bf16[8,4096]{1,0:T(8,128)(2,1)S(1)}, bf16[8,4096]{1,0:T(8,128)(2,1)S(1)}, u32[]{:S(2)}, u32[]{:S(2)}) collective-permute-start(bf16[8,4096]{1,0:T(8,128)(2,1)S(1)} %slice.155), channel_id=1, source_target_pairs={{0,8},{1,9},{2,10},{3,11},{4,12},{5,13},{6,14},{7,15},{8,0},{9,1},... | collective-permute-start | bytes 196616 | tf_op jit(solution)/shard_map/ppermute | solution.py:43
  55.3 1.0 collective-permute-done.14
  56.3 2.1 %collective-permute-start.18 = (bf16[8,4096]{1,0:T(8,128)(2,1)S(1)}, bf16[8,4096]{1,0:T(8,128)(2,1)S(1)}, u32[]{:S(2)}, u32[]{:S(2)}) collective-permute-start(bf16[8,4096]{1,0:T(8,128)(2,1)S(1)} %get-tuple-element.92), channel_id=1, source_target_pairs={{0,12},{1,13},{2,14},{3,15},{4,0},{5,1},{6,2},{7,3},{8,4},{9,5},{1... | collective-permute-start | bytes 196616 | tf_op jit(solution)/shard_map/ppermute | solution.py:43
  58.8 1.4 collective-permute-done.17
  60.2 3.9 %collective-permute-done.18 = bf16[8,4096]{1,0:T(8,128)(2,1)S(1)} collective-permute-done((bf16[8,4096]{1,0:T(8,128)(2,1)S(1)}, bf16[8,4096]{1,0:T(8,128)(2,1)S(1)}, u32[]{:S(2)}, u32[]{:S(2)}) %collective-permute-start.18) | collective-permute-done | bytes 65568 | tf_op jit(solution)/shard_map/ppermute | solution.py:43
  64.8 18.5 %all_to_all.10 = bf16[16,2,4096]{2,1,0:T(2,128)(2,1)S(1)} all-to-all(bf16[16,2,4096]{2,1,0:T(2,128)(2,1)S(1)} %reshape.26), channel_id=1, replica_groups=mesh['ctx'=16,'exp'=16] {'exp'}, dimensions={0} | all-to-all | bytes 524288 | tf_op jit(solution)/shard_map/all_to_all | solution.py:548
  83.3 0.6 fusion.23
  84.2 1.5 collective-permute-start.19
  85.7 2.2 %collective-permute-start.20 = (bf16[32,4096]{1,0:T(8,128)(2,1)S(1)}, bf16[32,4096]{1,0:T(8,128)(2,1)S(1)}, u32[]{:S(2)}, u32[]{:S(2)}) collective-permute-start(bf16[32,4096]{1,0:T(8,128)(2,1)S(1)} %pad_maximum_fusion.1), channel_id=1, source_target_pairs={{0,128},{1,33},{2,130},{3,35},{4,132},{5,37},{6,134},{7,39},{8,136... | collective-permute-start | bytes 786440 | tf_op jit(solution)/shard_map/ppermute | solution.py:455
  88.2 2.8 %collective-permute-done.19 = bf16[32,4096]{1,0:T(8,128)(2,1)S(1)} collective-permute-done((bf16[32,4096]{1,0:T(8,128)(2,1)S(1)}, bf16[32,4096]{1,0:T(8,128)(2,1)S(1)}, u32[]{:S(2)}, u32[]{:S(2)}) %collective-permute-start.19) | collective-permute-done | bytes 262176 | tf_op jit(solution)/shard_map/ppermute | solution.py:455
  91.0 3.7 %collective-permute-done.20 = bf16[32,4096]{1,0:T(8,128)(2,1)S(1)} collective-permute-done((bf16[32,4096]{1,0:T(8,128)(2,1)S(1)}, bf16[32,4096]{1,0:T(8,128)(2,1)S(1)}, u32[]{:S(2)}, u32[]{:S(2)}) %collective-permute-start.20) | collective-permute-done | bytes 262176 | tf_op jit(solution)/shard_map/ppermute | solution.py:455
  95.1 2.7 %collective-permute-start.26 = (bf16[64,4096]{1,0:T(8,128)(2,1)S(1)}, bf16[64,4096]{1,0:T(8,128)(2,1)S(1)}, u32[]{:S(2)}, u32[]{:S(2)}) collective-permute-start(bf16[64,4096]{1,0:T(8,128)(2,1)S(1)} %get-tuple-element.81), channel_id=1, source_target_pairs={{0,48},{1,193},{2,50},{3,195},{4,52},{5,197},{6,54},{7,199},{8,56}... | collective-permute-start | bytes 1572872 | tf_op jit(solution)/shard_map/ppermute | solution.py:455
  97.8 1.0 collective-permute-start.24
  98.8 2.3 %collective-permute-start.23 = (bf16[64,4096]{1,0:T(8,128)(2,1)S(1)}, bf16[64,4096]{1,0:T(8,128)(2,1)S(1)}, u32[]{:S(2)}, u32[]{:S(2)}) collective-permute-start(bf16[64,4096]{1,0:T(8,128)(2,1)S(1)} %get-tuple-element.82.refs_0_), channel_id=1, source_target_pairs={{0,48},{1,193},{2,50},{3,195},{4,52},{5,197},{6,54},{7,199},{8,56}... | collective-permute-start | bytes 1572872 | tf_op jit(solution)/shard_map/ppermute | solution.py:455
  101.1 3.5 %fetch.1 = (bf16[4096,512]{1,0:T(8,128)(2,1)S(1)}, bf16[512,4096]{1,0:T(8,128)(2,1)S(1)}) custom-call(bf16[128,4096]{1,0:T(8,128)(2,1)S(1)} %join.3.after_ref, bf16[4096,512]{1,0:T(8,128)(2,1)} %bitcast.16, bf16[512,4096]{1,0:T(8,128)(2,1)} %bitcast.17), custom_call_target="tpu_custom_call" | custom-call | bytes 33554432 | tf_op jit(solution)/shard_map/fetch/pallas_call | solution.py:424
  104.6 1.9 collective-permute-start.27
  106.4 4.0 %expert.3 = (bf16[64,4096]{1,0:T(8,128)(2,1)S(1)}, bf16[64,4096]{1,0:T(8,128)(2,1)S(1)}) custom-call(bf16[64,4096]{1,0:T(8,128)(2,1)S(1)} %get-tuple-element.82.refs_0_, bf16[64,4096]{1,0:T(8,128)(2,1)S(1)} %collective-permute-done.24.refs_1_, bf16[4096,512]{1,0:T(8,128)(2,1)S(1)} %get-tuple-element.63.refs_2_.refs_4_, ...), custom_call_target="tpu_custom_call" | custom-call | flops 1073741824 | bytes 2097152 | tf_op jit(solution)/shard_map/expert/pallas_call | solution.py:400
  110.5 0.6 collective-permute-start.28
  111.1 2.5 %collective-permute-start.29 = (bf16[64,4096]{1,0:T(8,128)(2,1)S(1)}, bf16[64,4096]{1,0:T(8,128)(2,1)S(1)}, u32[]{:S(2)}, u32[]{:S(2)}) collective-permute-start(bf16[64,4096]{1,0:T(8,128)(2,1)S(1)} %collective-permute-done.27.refs_3_), channel_id=1, source_target_pairs={{0,192},{1,49},{2,194},{3,51},{4,196},{5,53},{6,198},{7,55},{8,200... | collective-permute-start | bytes 1572872 | tf_op jit(solution)/shard_map/ppermute | solution.py:455
  113.6 1.6 collective-permute-start.25
  115.2 4.9 %collective-permute-done.28.refs_0_ = bf16[64,4096]{1,0:T(8,128)(2,1)S(1)} collective-permute-done((bf16[64,4096]{1,0:T(8,128)(2,1)S(1)}, bf16[64,4096]{1,0:T(8,128)(2,1)S(1)}, u32[]{:S(2)}, u32[]{:S(2)}) %collective-permute-start.28) | collective-permute-done | bytes 524320 | tf_op jit(solution)/shard_map/ppermute | solution.py:455
  120.1 4.0 %expert.5 = (bf16[64,4096]{1,0:T(8,128)(2,1)S(1)}, bf16[64,4096]{1,0:T(8,128)(2,1)S(1)}) custom-call(bf16[64,4096]{1,0:T(8,128)(2,1)S(1)} %collective-permute-done.28.refs_0_, bf16[64,4096]{1,0:T(8,128)(2,1)S(1)} %collective-permute-done.29.refs_1_, bf16[4096,512]{1,0:T(8,128)(2,1)S(1)} %get-tuple-element.63.refs_2_.refs_4_, ...), custom_call_target="tpu_custom_call" | custom-call | flops 1073741824 | bytes 2097152 | tf_op jit(solution)/shard_map/expert/pallas_call | solution.py:400
  124.1 1.8 collective-permute-start.30
  126.2 5.2 %expert.4 = (bf16[64,4096]{1,0:T(8,128)(2,1)S(1)}, bf16[64,4096]{1,0:T(8,128)(2,1)S(1)}, bf16[64,4096]{1,0:T(8,128)(2,1)S(1)}, bf16[64,4096]{1,0:T(8,128)(2,1)S(1)}) custom-call(bf16[64,4096]{1,0:T(8,128)(2,1)S(1)} %get-tuple-element.80.refs_0_, bf16[64,4096]{1,0:T(8,128)(2,1)S(1)} %collective-permute-done.23.refs_1_, ...), custom_call_target="tpu_custom_call" | custom-call | flops 2147483648 | bytes 4194304 | tf_op jit(solution)/shard_map/expert/pallas_call | solution.py:400
  131.3 3.5 %collective-permute-start.33 = (bf16[64,4096]{1,0:T(8,128)(2,1)S(1)}, bf16[64,4096]{1,0:T(8,128)(2,1)S(1)}, u32[]{:S(2)}, u32[]{:S(2)}) collective-permute-start(bf16[64,4096]{1,0:T(8,128)(2,1)S(1)} %get-tuple-element.70), channel_id=1, source_target_pairs={{0,1},{1,0},{2,3},{3,2},{4,5},{5,4},{6,7},{7,6},{8,9},{9,8},{10,11... | collective-permute-start | bytes 1572872 | tf_op jit(solution)/shard_map/ppermute | solution.py:43
  134.8 1.4 collective-permute-done.31
  136.3 3.5 %collective-permute-start.36 = (bf16[64,4096]{1,0:T(8,128)(2,1)S(1)}, bf16[64,4096]{1,0:T(8,128)(2,1)S(1)}, u32[]{:S(2)}, u32[]{:S(2)}) collective-permute-start(bf16[64,4096]{1,0:T(8,128)(2,1)S(1)} %add_convert_fusion.1), channel_id=1, source_target_pairs={{0,1},{1,0},{2,3},{3,2},{4,5},{5,4},{6,7},{7,6},{8,9},{9,8},{10,11... | collective-permute-start | bytes 1572872 | tf_op jit(solution)/shard_map/ppermute | solution.py:43
  140.0 1.8 collective-permute-start.34
  141.9 9.5 %collective-permute-done.35 = bf16[64,4096]{1,0:T(8,128)(2,1)S(1)} collective-permute-done((bf16[64,4096]{1,0:T(8,128)(2,1)S(1)}, bf16[64,4096]{1,0:T(8,128)(2,1)S(1)}, u32[]{:S(2)}, u32[]{:S(2)}) %collective-permute-start.35) | collective-permute-done | bytes 524320 | tf_op jit(solution)/shard_map/ppermute | solution.py:455
  151.4 5.6 %collective-permute-done.37 = bf16[64,4096]{1,0:T(8,128)(2,1)S(1)} collective-permute-done((bf16[64,4096]{1,0:T(8,128)(2,1)S(1)}, bf16[64,4096]{1,0:T(8,128)(2,1)S(1)}, u32[]{:S(2)}, u32[]{:S(2)}) %collective-permute-start.37) | collective-permute-done | bytes 524320 | tf_op jit(solution)/shard_map/ppermute | solution.py:455
  157.8 2.2 %collective-permute-start.39 = (bf16[32,4096]{1,0:T(8,128)(2,1)S(1)}, bf16[32,4096]{1,0:T(8,128)(2,1)S(1)}, u32[]{:S(2)}, u32[]{:S(2)}) collective-permute-start(bf16[32,4096]{1,0:T(8,128)(2,1)S(1)} %pad_maximum_fusion.3), channel_id=1, source_target_pairs={{0,128},{1,33},{2,130},{3,35},{4,132},{5,37},{6,134},{7,39},{8,136... | collective-permute-start | bytes 786440 | tf_op jit(solution)/shard_map/ppermute | solution.py:455
  160.0 0.7 collective-permute-start.38
  160.7 6.5 %collective-permute-done.40 = bf16[32,4096]{1,0:T(8,128)(2,1)S(1)} collective-permute-done((bf16[32,4096]{1,0:T(8,128)(2,1)S(1)}, bf16[32,4096]{1,0:T(8,128)(2,1)S(1)}, u32[]{:S(2)}, u32[]{:S(2)}) %collective-permute-start.40) | collective-permute-done | bytes 262176 | tf_op jit(solution)/shard_map/ppermute | solution.py:455
  167.3 0.7 collective-permute-done.38
  168.2 1.0 copy.47
  169.2 5.1 %all-to-all-start.1 = ((bf16[16,2,4096]{2,1,0:T(2,128)(2,1)}), bf16[16,2,4096]{2,1,0:T(2,128)(2,1)S(1)}, u32[]{:S(2)}, u32[]{:S(2)}) async-start(bf16[16,2,4096]{2,1,0:T(2,128)(2,1)} %copy.47), calls=%async_computation.1 | async-start | bytes 524288 | tf_op jit(solution)/shard_map/all_to_all | solution.py:551
  174.4 11.7 %all-to-all-done.1 = bf16[16,2,4096]{2,1,0:T(2,128)(2,1)S(1)} async-done(((bf16[16,2,4096]{2,1,0:T(2,128)(2,1)}), bf16[16,2,4096]{2,1,0:T(2,128)(2,1)S(1)}, u32[]{:S(2)}, u32[]{:S(2)}) %all-to-all-start.1) | async-done | bytes 262176 | tf_op jit(solution)/shard_map/all_to_all | solution.py:551
  186.2 0.9 fusion
  (85 shorter events, 5.5 us)
Async XLA Ops:
  0.0 47.7 %copy-start.2 = (s32[8,2]{0,1:T(2,128)S(1)}, s32[8,2]{0,1:T(2,128)}, u32[]{:S(2)}) copy-start(s32[8,2]{0,1:T(2,128)} %param.26) | copy-start | bytes 196
  0.7 5.4 %collective-permute-start = (bf16[3,512]{1,0:T(4,128)(2,1)S(1)}, bf16[3,512]{1,0:T(4,128)(2,1)S(1)}, u32[]{:S(2)}, u32[]{:S(2)}) collective-permute-start(bf16[3,512]{1,0:T(4,128)(2,1)S(1)} %slice.113), channel_id=1, source_target_pairs={{0,16},{16,32},{32,48},{48,64},{64,80},{80,96},{96,112},{112,128},... | collective-permute-start | bytes 9224 | tf_op jit(solution)/shard_map/ppermute | solution.py:25
  6.3 3.9 %collective-permute-start.3 = (f32[32,128]{1,0:T(8,128)S(1)}, f32[32,128]{1,0:T(8,128)S(1)}, u32[]{:S(2)}, u32[]{:S(2)}) collective-permute-start(f32[32,128]{1,0:T(8,128)S(1)} %get-tuple-element.44), channel_id=1, source_target_pairs={{0,3},{1,2},{2,1},{3,0},{4,7},{5,6},{6,5},{7,4},{8,11},{9,10},{10,... | collective-permute-start | bytes 49160 | tf_op jit(solution)/shard_map/ppermute | solution.py:43
  8.8 3.0 %collective-permute-start.2 = (f32[32,128]{1,0:T(8,128)S(1)}, f32[32,128]{1,0:T(8,128)S(1)}, u32[]{:S(2)}, u32[]{:S(2)}) collective-permute-start(f32[32,128]{1,0:T(8,128)S(1)} %get-tuple-element.44), channel_id=1, source_target_pairs={{0,2},{1,3},{2,0},{3,1},{4,6},{5,7},{6,4},{7,5},{8,10},{9,11},{10,... | collective-permute-start | bytes 49160 | tf_op jit(solution)/shard_map/ppermute | solution.py:43
  8.8 3.0 %collective-permute-start.1 = (f32[32,128]{1,0:T(8,128)S(1)}, f32[32,128]{1,0:T(8,128)S(1)}, u32[]{:S(2)}, u32[]{:S(2)}) collective-permute-start(f32[32,128]{1,0:T(8,128)S(1)} %get-tuple-element.44), channel_id=1, source_target_pairs={{0,1},{1,0},{2,3},{3,2},{4,5},{5,4},{6,7},{7,6},{8,9},{9,8},{10,11... | collective-permute-start | bytes 49160 | tf_op jit(solution)/shard_map/ppermute | solution.py:43
  11.8 9.7 %collective-permute-start.4 = (f32[32,128]{1,0:T(8,128)S(1)}, f32[32,128]{1,0:T(8,128)S(1)}, u32[]{:S(2)}, u32[]{:S(2)}) collective-permute-start(f32[32,128]{1,0:T(8,128)S(1)} %add_add_fusion.a_ref), channel_id=1, source_target_pairs={{0,4},{1,5},{2,6},{3,7},{4,8},{5,9},{6,10},{7,11},{8,12},{9,13},{1... | collective-permute-start | bytes 49160 | tf_op jit(solution)/shard_map/ppermute | solution.py:43
  14.9 6.6 %collective-permute-start.5 = (f32[32,128]{1,0:T(8,128)S(1)}, f32[32,128]{1,0:T(8,128)S(1)}, u32[]{:S(2)}, u32[]{:S(2)}) collective-permute-start(f32[32,128]{1,0:T(8,128)S(1)} %add_add_fusion.a_ref), channel_id=1, source_target_pairs={{0,8},{1,9},{2,10},{3,11},{4,12},{5,13},{6,14},{7,15},{8,0},{9,1},... | collective-permute-start | bytes 49160 | tf_op jit(solution)/shard_map/ppermute | solution.py:43
  19.1 3.7 %collective-permute-start.6 = (f32[32,128]{1,0:T(8,128)S(1)}, f32[32,128]{1,0:T(8,128)S(1)}, u32[]{:S(2)}, u32[]{:S(2)}) collective-permute-start(f32[32,128]{1,0:T(8,128)S(1)} %add_add_fusion.a_ref), channel_id=1, source_target_pairs={{0,12},{1,13},{2,14},{3,15},{4,0},{5,1},{6,2},{7,3},{8,4},{9,5},{1... | collective-permute-start | bytes 49160 | tf_op jit(solution)/shard_map/ppermute | solution.py:43
  24.0 5.4 %collective-permute-start.7 = (bf16[32,512]{1,0:T(8,128)(2,1)S(1)}, bf16[32,512]{1,0:T(8,128)(2,1)S(1)}, u32[]{:S(2)}, u32[]{:S(2)}) collective-permute-start(bf16[32,512]{1,0:T(8,128)(2,1)S(1)} %get-tuple-element.47.a_ref), channel_id=1, source_target_pairs={{0,16},{16,32},{32,48},{48,0},{64,80},{80,96},{96,112},{112,64},{1... | collective-permute-start | bytes 98312 | tf_op jit(solution)/shard_map/ppermute | solution.py:34
  25.7 4.3 %collective-permute-start.8 = (bf16[32,512]{1,0:T(8,128)(2,1)S(1)}, bf16[32,512]{1,0:T(8,128)(2,1)S(1)}, u32[]{:S(2)}, u32[]{:S(2)}) collective-permute-start(bf16[32,512]{1,0:T(8,128)(2,1)S(1)} %get-tuple-element.47.a_ref), channel_id=1, source_target_pairs={{0,32},{16,48},{32,0},{48,16},{64,96},{80,112},{96,64},{112,80},{1... | collective-permute-start | bytes 98312 | tf_op jit(solution)/shard_map/ppermute | solution.py:34
  28.4 2.8 %collective-permute-start.9 = (bf16[32,512]{1,0:T(8,128)(2,1)S(1)}, bf16[32,512]{1,0:T(8,128)(2,1)S(1)}, u32[]{:S(2)}, u32[]{:S(2)}) collective-permute-start(bf16[32,512]{1,0:T(8,128)(2,1)S(1)} %get-tuple-element.47.a_ref), channel_id=1, source_target_pairs={{0,48},{16,0},{32,16},{48,32},{64,112},{80,64},{96,80},{112,96},{1... | collective-permute-start | bytes 98312 | tf_op jit(solution)/shard_map/ppermute | solution.py:34
  31.3 5.2 %collective-permute-start.10 = (bf16[32,512]{1,0:T(8,128)(2,1)S(1)}, bf16[32,512]{1,0:T(8,128)(2,1)S(1)}, u32[]{:S(2)}, u32[]{:S(2)}) collective-permute-start(bf16[32,512]{1,0:T(8,128)(2,1)S(1)} %get-tuple-element.48.refs_0_), channel_id=1, source_target_pairs={{0,64},{16,80},{32,96},{48,112},{64,128},{80,144},{96,160},{112,17... | collective-permute-start | bytes 98312 | tf_op jit(solution)/shard_map/ppermute | solution.py:34
  32.9 4.3 %collective-permute-start.11 = (bf16[32,512]{1,0:T(8,128)(2,1)S(1)}, bf16[32,512]{1,0:T(8,128)(2,1)S(1)}, u32[]{:S(2)}, u32[]{:S(2)}) collective-permute-start(bf16[32,512]{1,0:T(8,128)(2,1)S(1)} %get-tuple-element.48.refs_0_), channel_id=1, source_target_pairs={{0,128},{16,144},{32,160},{48,176},{64,192},{80,208},{96,224},{112... | collective-permute-start | bytes 98312 | tf_op jit(solution)/shard_map/ppermute | solution.py:34
  35.3 2.8 %collective-permute-start.12 = (bf16[32,512]{1,0:T(8,128)(2,1)S(1)}, bf16[32,512]{1,0:T(8,128)(2,1)S(1)}, u32[]{:S(2)}, u32[]{:S(2)}) collective-permute-start(bf16[32,512]{1,0:T(8,128)(2,1)S(1)} %get-tuple-element.48.refs_0_), channel_id=1, source_target_pairs={{0,192},{16,208},{32,224},{48,240},{64,0},{80,16},{96,32},{112,48}... | collective-permute-start | bytes 98312 | tf_op jit(solution)/shard_map/ppermute | solution.py:34
  38.1 26.0 %copy-start = (bf16[8,4096]{1,0:T(8,128)(2,1)S(1)}, bf16[8,4096]{1,0:T(8,128)(2,1)}, u32[]{:S(2)}) copy-start(bf16[8,4096]{1,0:T(8,128)(2,1)} %param.24) | copy-start | bytes 196612
  38.1 26.2 %copy-start.1 = (f32[4096]{0:T(1024)S(1)}, f32[4096]{0:T(1024)}, u32[]{:S(2)}) copy-start(f32[4096]{0:T(1024)} %param.25) | copy-start | bytes 49156
  42.4 6.9 %collective-permute-start.13 = (bf16[64,4096]{1,0:T(8,128)(2,1)S(1)}, bf16[64,4096]{1,0:T(8,128)(2,1)S(1)}, u32[]{:S(2)}, u32[]{:S(2)}) collective-permute-start(bf16[64,4096]{1,0:T(8,128)(2,1)S(1)} %get-tuple-element.55), channel_id=1, source_target_pairs={{0,1},{1,0},{2,3},{3,2},{4,5},{5,4},{6,7},{7,6},{8,9},{9,8},{10,11... | collective-permute-start | bytes 1572872 | tf_op jit(solution)/shard_map/ppermute | solution.py:43
  49.4 6.8 %collective-permute-start.14 = (bf16[16,4096]{1,0:T(8,128)(2,1)S(1)}, bf16[16,4096]{1,0:T(8,128)(2,1)S(1)}, u32[]{:S(2)}, u32[]{:S(2)}) collective-permute-start(bf16[16,4096]{1,0:T(8,128)(2,1)S(1)} %get-tuple-element.93), channel_id=1, source_target_pairs={{0,2},{1,3},{2,4},{3,5},{4,6},{5,7},{6,8},{7,9},{8,10},{9,11},{10,... | collective-permute-start | bytes 393224 | tf_op jit(solution)/shard_map/ppermute | solution.py:43
  50.2 6.0 %collective-permute-start.15 = (bf16[16,4096]{1,0:T(8,128)(2,1)S(1)}, bf16[16,4096]{1,0:T(8,128)(2,1)S(1)}, u32[]{:S(2)}, u32[]{:S(2)}) collective-permute-start(bf16[16,4096]{1,0:T(8,128)(2,1)S(1)} %get-tuple-element.94), channel_id=1, source_target_pairs={{0,14},{1,15},{2,0},{3,1},{4,2},{5,3},{6,4},{7,5},{8,6},{9,7},{10,... | collective-permute-start | bytes 393224 | tf_op jit(solution)/shard_map/ppermute | solution.py:43
  52.9 7.3 %collective-permute-start.17 = (bf16[8,4096]{1,0:T(8,128)(2,1)S(1)}, bf16[8,4096]{1,0:T(8,128)(2,1)S(1)}, u32[]{:S(2)}, u32[]{:S(2)}) collective-permute-start(bf16[8,4096]{1,0:T(8,128)(2,1)S(1)} %slice.155), channel_id=1, source_target_pairs={{0,8},{1,9},{2,10},{3,11},{4,12},{5,13},{6,14},{7,15},{8,0},{9,1},... | collective-permute-start | bytes 196616 | tf_op jit(solution)/shard_map/ppermute | solution.py:43
  56.3 7.8 %collective-permute-start.18 = (bf16[8,4096]{1,0:T(8,128)(2,1)S(1)}, bf16[8,4096]{1,0:T(8,128)(2,1)S(1)}, u32[]{:S(2)}, u32[]{:S(2)}) collective-permute-start(bf16[8,4096]{1,0:T(8,128)(2,1)S(1)} %get-tuple-element.92), channel_id=1, source_target_pairs={{0,12},{1,13},{2,14},{3,15},{4,0},{5,1},{6,2},{7,3},{8,4},{9,5},{1... | collective-permute-start | bytes 196616 | tf_op jit(solution)/shard_map/ppermute | solution.py:43
  58.3 5.7 %collective-permute-start.16 = (bf16[8,4096]{1,0:T(8,128)(2,1)S(1)}, bf16[8,4096]{1,0:T(8,128)(2,1)S(1)}, u32[]{:S(2)}, u32[]{:S(2)}) collective-permute-start(bf16[8,4096]{1,0:T(8,128)(2,1)S(1)} %get-tuple-element.91), channel_id=1, source_target_pairs={{0,4},{1,5},{2,6},{3,7},{4,8},{5,9},{6,10},{7,11},{8,12},{9,13},{1... | collective-permute-start | bytes 196616 | tf_op jit(solution)/shard_map/ppermute | solution.py:43
  84.2 6.8 %collective-permute-start.19 = (bf16[32,4096]{1,0:T(8,128)(2,1)S(1)}, bf16[32,4096]{1,0:T(8,128)(2,1)S(1)}, u32[]{:S(2)}, u32[]{:S(2)}) collective-permute-start(bf16[32,4096]{1,0:T(8,128)(2,1)S(1)} %pad_maximum_fusion.1), channel_id=1, source_target_pairs={{0,64},{1,17},{2,66},{3,19},{4,68},{5,21},{6,70},{7,23},{8,72},{9,... | collective-permute-start | bytes 786440 | tf_op jit(solution)/shard_map/ppermute | solution.py:455
  85.7 9.1 %collective-permute-start.20 = (bf16[32,4096]{1,0:T(8,128)(2,1)S(1)}, bf16[32,4096]{1,0:T(8,128)(2,1)S(1)}, u32[]{:S(2)}, u32[]{:S(2)}) collective-permute-start(bf16[32,4096]{1,0:T(8,128)(2,1)S(1)} %pad_maximum_fusion.1), channel_id=1, source_target_pairs={{0,128},{1,33},{2,130},{3,35},{4,132},{5,37},{6,134},{7,39},{8,136... | collective-permute-start | bytes 786440 | tf_op jit(solution)/shard_map/ppermute | solution.py:455
  87.9 6.9 %collective-permute-start.21 = (bf16[32,4096]{1,0:T(8,128)(2,1)S(1)}, bf16[32,4096]{1,0:T(8,128)(2,1)S(1)}, u32[]{:S(2)}, u32[]{:S(2)}) collective-permute-start(bf16[32,4096]{1,0:T(8,128)(2,1)S(1)} %pad_maximum_fusion.1), channel_id=1, source_target_pairs={{0,192},{1,49},{2,194},{3,51},{4,196},{5,53},{6,198},{7,55},{8,200... | collective-permute-start | bytes 786440 | tf_op jit(solution)/shard_map/ppermute | solution.py:455
  94.9 15.5 %collective-permute-start.22 = (bf16[128,4096]{1,0:T(8,128)(2,1)S(1)}, bf16[128,4096]{1,0:T(8,128)(2,1)S(1)}, u32[]{:S(2)}, u32[]{:S(2)}) collective-permute-start(bf16[128,4096]{1,0:T(8,128)(2,1)S(1)} %join.3.after_ref), channel_id=1, source_target_pairs={{0,16},{1,65},{2,18},{3,67},{4,20},{5,69},{6,22},{7,71},{8,24},{9,... | collective-permute-start | bytes 3145736 | tf_op jit(solution)/shard_map/ppermute | solution.py:455
  95.1 9.5 %collective-permute-start.26 = (bf16[64,4096]{1,0:T(8,128)(2,1)S(1)}, bf16[64,4096]{1,0:T(8,128)(2,1)S(1)}, u32[]{:S(2)}, u32[]{:S(2)}) collective-permute-start(bf16[64,4096]{1,0:T(8,128)(2,1)S(1)} %get-tuple-element.81), channel_id=1, source_target_pairs={{0,48},{1,193},{2,50},{3,195},{4,52},{5,197},{6,54},{7,199},{8,56}... | collective-permute-start | bytes 1572872 | tf_op jit(solution)/shard_map/ppermute | solution.py:455
  97.8 8.6 %collective-permute-start.24 = (bf16[64,4096]{1,0:T(8,128)(2,1)S(1)}, bf16[64,4096]{1,0:T(8,128)(2,1)S(1)}, u32[]{:S(2)}, u32[]{:S(2)}) collective-permute-start(bf16[64,4096]{1,0:T(8,128)(2,1)S(1)} %get-tuple-element.81), channel_id=1, source_target_pairs={{0,1},{1,0},{2,3},{3,2},{4,5},{5,4},{6,7},{7,6},{8,9},{9,8},{10,11... | collective-permute-start | bytes 1572872 | tf_op jit(solution)/shard_map/ppermute | solution.py:43
  98.8 11.6 %collective-permute-start.23 = (bf16[64,4096]{1,0:T(8,128)(2,1)S(1)}, bf16[64,4096]{1,0:T(8,128)(2,1)S(1)}, u32[]{:S(2)}, u32[]{:S(2)}) collective-permute-start(bf16[64,4096]{1,0:T(8,128)(2,1)S(1)} %get-tuple-element.82.refs_0_), channel_id=1, source_target_pairs={{0,48},{1,193},{2,50},{3,195},{4,52},{5,197},{6,54},{7,199},{8,56}... | collective-permute-start | bytes 1572872 | tf_op jit(solution)/shard_map/ppermute | solution.py:455
  104.6 6.6 %collective-permute-start.27 = (bf16[64,4096]{1,0:T(8,128)(2,1)S(1)}, bf16[64,4096]{1,0:T(8,128)(2,1)S(1)}, u32[]{:S(2)}, u32[]{:S(2)}) collective-permute-start(bf16[64,4096]{1,0:T(8,128)(2,1)S(1)} %collective-permute-done.26), channel_id=1, source_target_pairs={{0,1},{1,0},{2,3},{3,2},{4,5},{5,4},{6,7},{7,6},{8,9},{9,8},{10,11... | collective-permute-start | bytes 1572872 | tf_op jit(solution)/shard_map/ppermute | solution.py:43
  110.5 9.6 %collective-permute-start.28 = (bf16[64,4096]{1,0:T(8,128)(2,1)S(1)}, bf16[64,4096]{1,0:T(8,128)(2,1)S(1)}, u32[]{:S(2)}, u32[]{:S(2)}) collective-permute-start(bf16[64,4096]{1,0:T(8,128)(2,1)S(1)} %get-tuple-element.80.refs_0_), channel_id=1, source_target_pairs={{0,16},{1,65},{2,18},{3,67},{4,20},{5,69},{6,22},{7,71},{8,24},{9,... | collective-permute-start | bytes 1572872 | tf_op jit(solution)/shard_map/ppermute | solution.py:455
  111.1 9.0 %collective-permute-start.29 = (bf16[64,4096]{1,0:T(8,128)(2,1)S(1)}, bf16[64,4096]{1,0:T(8,128)(2,1)S(1)}, u32[]{:S(2)}, u32[]{:S(2)}) collective-permute-start(bf16[64,4096]{1,0:T(8,128)(2,1)S(1)} %collective-permute-done.27.refs_3_), channel_id=1, source_target_pairs={{0,192},{1,49},{2,194},{3,51},{4,196},{5,53},{6,198},{7,55},{8,200... | collective-permute-start | bytes 1572872 | tf_op jit(solution)/shard_map/ppermute | solution.py:455
  113.6 12.5 %collective-permute-start.25 = (bf16[64,4096]{1,0:T(8,128)(2,1)S(1)}, bf16[64,4096]{1,0:T(8,128)(2,1)S(1)}, u32[]{:S(2)}, u32[]{:S(2)}) collective-permute-start(bf16[64,4096]{1,0:T(8,128)(2,1)S(1)} %get-tuple-element.79), channel_id=1, source_target_pairs={{0,1},{1,0},{2,3},{3,2},{4,5},{5,4},{6,7},{7,6},{8,9},{9,8},{10,11... | collective-permute-start | bytes 1572872 | tf_op jit(solution)/shard_map/ppermute | solution.py:43
  115.2 19.5 %collective-permute-start.32 = (bf16[64,4096]{1,0:T(8,128)(2,1)S(1)}, bf16[64,4096]{1,0:T(8,128)(2,1)S(1)}, u32[]{:S(2)}, u32[]{:S(2)}) collective-permute-start(bf16[64,4096]{1,0:T(8,128)(2,1)S(1)} %get-tuple-element.68), channel_id=1, source_target_pairs={{0,1},{1,0},{2,3},{3,2},{4,5},{5,4},{6,7},{7,6},{8,9},{9,8},{10,11... | collective-permute-start | bytes 1572872 | tf_op jit(solution)/shard_map/ppermute | solution.py:43
  124.1 10.7 %collective-permute-start.30 = (bf16[64,4096]{1,0:T(8,128)(2,1)S(1)}, bf16[64,4096]{1,0:T(8,128)(2,1)S(1)}, u32[]{:S(2)}, u32[]{:S(2)}) collective-permute-start(bf16[64,4096]{1,0:T(8,128)(2,1)S(1)} %get-tuple-element.66), channel_id=1, source_target_pairs={{0,48},{1,193},{2,50},{3,195},{4,52},{5,197},{6,54},{7,199},{8,56}... | collective-permute-start | bytes 1572872 | tf_op jit(solution)/shard_map/ppermute | solution.py:455
  125.9 10.3 %collective-permute-start.31 = (bf16[64,4096]{1,0:T(8,128)(2,1)S(1)}, bf16[64,4096]{1,0:T(8,128)(2,1)S(1)}, u32[]{:S(2)}, u32[]{:S(2)}) collective-permute-start(bf16[64,4096]{1,0:T(8,128)(2,1)S(1)} %get-tuple-element.67), channel_id=1, source_target_pairs={{0,64},{1,17},{2,66},{3,19},{4,68},{5,21},{6,70},{7,23},{8,72},{9,... | collective-permute-start | bytes 1572872 | tf_op jit(solution)/shard_map/ppermute | solution.py:455
  131.3 8.6 %collective-permute-start.33 = (bf16[64,4096]{1,0:T(8,128)(2,1)S(1)}, bf16[64,4096]{1,0:T(8,128)(2,1)S(1)}, u32[]{:S(2)}, u32[]{:S(2)}) collective-permute-start(bf16[64,4096]{1,0:T(8,128)(2,1)S(1)} %get-tuple-element.70), channel_id=1, source_target_pairs={{0,1},{1,0},{2,3},{3,2},{4,5},{5,4},{6,7},{7,6},{8,9},{9,8},{10,11... | collective-permute-start | bytes 1572872 | tf_op jit(solution)/shard_map/ppermute | solution.py:43
  136.3 5.6 %collective-permute-start.36 = (bf16[64,4096]{1,0:T(8,128)(2,1)S(1)}, bf16[64,4096]{1,0:T(8,128)(2,1)S(1)}, u32[]{:S(2)}, u32[]{:S(2)}) collective-permute-start(bf16[64,4096]{1,0:T(8,128)(2,1)S(1)} %add_convert_fusion.1), channel_id=1, source_target_pairs={{0,1},{1,0},{2,3},{3,2},{4,5},{5,4},{6,7},{7,6},{8,9},{9,8},{10,11... | collective-permute-start | bytes 1572872 | tf_op jit(solution)/shard_map/ppermute | solution.py:43
  140.0 17.0 %collective-permute-start.34 = (bf16[128,4096]{1,0:T(8,128)(2,1)S(1)}, bf16[128,4096]{1,0:T(8,128)(2,1)S(1)}, u32[]{:S(2)}, u32[]{:S(2)}) collective-permute-start(bf16[128,4096]{1,0:T(8,128)(2,1)S(1)} %pad_maximum_fusion), channel_id=1, source_target_pairs={{0,48},{1,193},{2,50},{3,195},{4,52},{5,197},{6,54},{7,199},{8,56}... | collective-permute-start | bytes 3145736 | tf_op jit(solution)/shard_map/ppermute | solution.py:455
  141.9 9.5 %collective-permute-start.35 = (bf16[64,4096]{1,0:T(8,128)(2,1)S(1)}, bf16[64,4096]{1,0:T(8,128)(2,1)S(1)}, u32[]{:S(2)}, u32[]{:S(2)}) collective-permute-start(bf16[64,4096]{1,0:T(8,128)(2,1)S(1)} %get-tuple-element.71), channel_id=1, source_target_pairs={{0,16},{1,65},{2,18},{3,67},{4,20},{5,69},{6,22},{7,71},{8,24},{9,... | collective-permute-start | bytes 1572872 | tf_op jit(solution)/shard_map/ppermute | solution.py:455
  141.9 15.1 %collective-permute-start.37 = (bf16[64,4096]{1,0:T(8,128)(2,1)S(1)}, bf16[64,4096]{1,0:T(8,128)(2,1)S(1)}, u32[]{:S(2)}, u32[]{:S(2)}) collective-permute-start(bf16[64,4096]{1,0:T(8,128)(2,1)S(1)} %collective-permute-done.36), channel_id=1, source_target_pairs={{0,16},{1,65},{2,18},{3,67},{4,20},{5,69},{6,22},{7,71},{8,24},{9,... | collective-permute-start | bytes 1572872 | tf_op jit(solution)/shard_map/ppermute | solution.py:455
  157.5 16.8 %copy-start.3 = (s32[8,2]{0,1:T(2,128)S(1)}, s32[8,2]{0,1:T(2,128)}, u32[]{:S(2)}) copy-start(s32[8,2]{0,1:T(2,128)} %param.27) | copy-start | bytes 196
  157.6 9.6 %collective-permute-start.40 = (bf16[32,4096]{1,0:T(8,128)(2,1)S(1)}, bf16[32,4096]{1,0:T(8,128)(2,1)S(1)}, u32[]{:S(2)}, u32[]{:S(2)}) collective-permute-start(bf16[32,4096]{1,0:T(8,128)(2,1)S(1)} %pad_maximum_fusion.4), channel_id=1, source_target_pairs={{0,64},{1,17},{2,66},{3,19},{4,68},{5,21},{6,70},{7,23},{8,72},{9,... | collective-permute-start | bytes 786440 | tf_op jit(solution)/shard_map/ppermute | solution.py:455
  157.8 9.5 %collective-permute-start.39 = (bf16[32,4096]{1,0:T(8,128)(2,1)S(1)}, bf16[32,4096]{1,0:T(8,128)(2,1)S(1)}, u32[]{:S(2)}, u32[]{:S(2)}) collective-permute-start(bf16[32,4096]{1,0:T(8,128)(2,1)S(1)} %pad_maximum_fusion.3), channel_id=1, source_target_pairs={{0,128},{1,33},{2,130},{3,35},{4,132},{5,37},{6,134},{7,39},{8,136... | collective-permute-start | bytes 786440 | tf_op jit(solution)/shard_map/ppermute | solution.py:455
  160.0 8.0 %collective-permute-start.38 = (bf16[32,4096]{1,0:T(8,128)(2,1)S(1)}, bf16[32,4096]{1,0:T(8,128)(2,1)S(1)}, u32[]{:S(2)}, u32[]{:S(2)}) collective-permute-start(bf16[32,4096]{1,0:T(8,128)(2,1)S(1)} %pad_maximum_fusion.2), channel_id=1, source_target_pairs={{0,192},{1,49},{2,194},{3,51},{4,196},{5,53},{6,198},{7,55},{8,200... | collective-permute-start | bytes 786440 | tf_op jit(solution)/shard_map/ppermute | solution.py:455
  169.2 16.9 %all-to-all-start.1 = ((bf16[16,2,4096]{2,1,0:T(2,128)(2,1)}), bf16[16,2,4096]{2,1,0:T(2,128)(2,1)S(1)}, u32[]{:S(2)}, u32[]{:S(2)}) async-start(bf16[16,2,4096]{2,1,0:T(2,128)(2,1)} %copy.47), calls=%async_computation.1 | async-start | bytes 524288 | tf_op jit(solution)/shard_map/all_to_all | solution.py:551
